TPU v7x, 32 devices: a whole 2x2x4 slice. The times are simulated.
32 devices in a mesh: dp: 8 (over y, x, core), group: 4 (over z).
Axes of the slice: x: 2, y: 2, z: 4, core: 2. Of those that a mesh axis runs over, the one named last changes fastest.
Arguments:
- tokens: float32 [6304, 768], P(('dp', 'group')), may hold values from -6 to 6
- cotangent: float32 [6304, 768], P(('dp', 'group')), may hold values from -6 to 6
- expert_ids: int32 [6304, 2], P(('dp', 'group')), may hold values from 0 to 15, as said below
- slot_pos: int32 [6304, 2], P(('dp', 'group')), may hold values from -1 to 24, as said below
- qkv_w: float32 [768, 2304], P(('dp', 'group')), may hold values from -0.21875 to 0.21875
- qkv_m: float32 [768, 2304], P(('dp', 'group')), may hold values from -18 to 18
- qkv_v: float32 [768, 2304], P(('dp', 'group')), may hold values from 0.3 to 3
- out_w: float32 [768, 768], P(('dp', 'group')), may hold values from -0.875 to 0.875
- out_m: float32 [768, 768], P(('dp', 'group')), may hold values from -18 to 18
- out_v: float32 [768, 768], P(('dp', 'group')), may hold values from 0.3 to 3
- vectors: float32 [39, 768], P(None, ('dp', 'group'))
- vec_m: float32 [39, 768], P(None, ('dp', 'group')), may hold values from -120 to 120
- vec_v: float32 [39, 768], P(None, ('dp', 'group')), may hold values from 40 to 4000
- w_in: float32 [768, 49152], P('group', 'dp'), may hold values from -0.21875 to 0.21875
- w_in_m: float32 [768, 49152], P('group', 'dp'), may hold values from -15 to 15
- w_in_v: float32 [768, 49152], P('group', 'dp'), may hold values from 0.17 to 1.7
- w_out: float32 [49152, 768], P('dp', 'group'), may hold values from -0.875 to 0.875
- w_out_m: float32 [49152, 768], P('dp', 'group'), may hold values from -4 to 4
- w_out_v: float32 [49152, 768], P('dp', 'group'), may hold values from 0.01 to 0.1
- b_in: float32 [49152], P(('dp', 'group')), may hold values from -3 to 3
- b_in_m: float32 [49152], P(('dp', 'group')), may hold values from -15 to 15
- b_in_v: float32 [49152], P(('dp', 'group')), may hold values from 0.17 to 1.7
Outputs:
- block_out: float32 [6304, 768], P(('dp', 'group'))
- input_grad: float32 [6304, 768], P(('dp', 'group'))
- qkv_grad: float32 [768, 2304], P(('dp', 'group'))
- qkv_new: float32 [768, 2304], P(('dp', 'group'))
- qkv_m_new: float32 [768, 2304], P(('dp', 'group'))
- qkv_v_new: float32 [768, 2304], P(('dp', 'group'))
- out_grad: float32 [768, 768], P(('dp', 'group'))
- out_new: float32 [768, 768], P(('dp', 'group'))
- out_m_new: float32 [768, 768], P(('dp', 'group'))
- out_v_new: float32 [768, 768], P(('dp', 'group'))
- vec_grad: float32 [39, 768], P(None, ('dp', 'group'))
- vec_new: float32 [39, 768], P(None, ('dp', 'group'))
- vec_m_new: float32 [39, 768], P(None, ('dp', 'group'))
- vec_v_new: float32 [39, 768], P(None, ('dp', 'group'))
- w_in_grad: float32 [768, 49152], P('group', 'dp')
- w_in_new: float32 [768, 49152], P('group', 'dp')
- w_in_m_new: float32 [768, 49152], P('group', 'dp')
- w_in_v_new: float32 [768, 49152], P('group', 'dp')
- w_out_grad: float32 [49152, 768], P('dp', 'group')
- w_out_new: float32 [49152, 768], P('dp', 'group')
- w_out_m_new: float32 [49152, 768], P('dp', 'group')
- w_out_v_new: float32 [49152, 768], P('dp', 'group')
- b_in_grad: float32 [49152], P(('dp', 'group'))
- b_in_new: float32 [49152], P(('dp', 'group'))
- b_in_m_new: float32 [49152], P(('dp', 'group'))
- b_in_v_new: float32 [49152], P(('dp', 'group'))
- branch_bias_grad: float32 [17, 768], P(None, ('dp', 'group'))
Inputs may be any that keep to these rules, and one draw needn't show every extreme that they name: `expert_ids`: each row names two different experts. `slot_pos`: the slot of a choice in its expert's buffer for its aligned block of 197 rows; slots of one expert within a block are distinct; -1 marks a dropped choice; in every block some expert fills all 25 slots.
All inputs are finite; a program needn't handle non-finite values.
Results may differ from a plain program's by a relative error of at most 0.018.
Values may be sent and summed in bfloat16 or wider, within the bound.
No kernel may reach another device: no remote copies, remote signals or barrier semaphores. Data moves between devices by JAX's collectives and lax.ppermute only.
A program may use at most 256 MiB of HBM per device.

v0:
```python
import jax
import jax.numpy as jnp
from jax import lax
from jax.sharding import PartitionSpec as P

D = 768
HEADS = 12
HEAD = 64
FF = 3072
EXPERTS = 16
SEQ = 197
CAP = 25


LEARN_RATE = 0.15
BETA_ONE = 0.9
BETA_TWO = 0.999
ADAM_EPS = 1e-08
WEIGHT_DECAY = 0.1
CORR_ONE = 1.0 - BETA_ONE**2
CORR_TWO = 1.0 - BETA_TWO**2
NORM_EPS = 1e-06
EXACT = lax.Precision.HIGHEST


def to_half(values):
    return values.astype(jnp.bfloat16)


def heads_split(values):
    return values.reshape(-1, SEQ, HEADS, HEAD)


def normalize(values):
    average = jnp.mean(values, axis=-1, keepdims=True)
    centered = values - average
    inv_std = lax.rsqrt(jnp.mean(centered * centered, axis=-1, keepdims=True) + NORM_EPS)
    return (centered * inv_std, inv_std)


def normalize_back(grad_norm, normed, inv_std):
    return inv_std * (
        grad_norm
        - jnp.mean(grad_norm, axis=-1, keepdims=True)
        - normed * jnp.mean(grad_norm * normed, axis=-1, keepdims=True)
    )


def expert_table(ids_here):
    return (ids_here[..., None] == jnp.arange(EXPERTS)[None, None, :]).astype(jnp.float32)


def slot_table(ids_here, slots_here):
    kept_mask = slots_here >= 0
    target = ids_here * CAP + slots_here
    slot_hits = (target[..., None] == jnp.arange(EXPERTS * CAP)[None, None, :]) & kept_mask[
        ..., None
    ]
    return (slot_hits.astype(jnp.float32), kept_mask)


def select_rows(results, ids_here, slots_here):
    kept_mask = slots_here >= 0
    flat_index = jnp.where(kept_mask, ids_here * CAP + slots_here, 0)
    return (jnp.take(results, flat_index, axis=0), kept_mask)


def forward_rows(row_block, qkv_half, out_half, vec_real, router_half):
    normed_one, inv_one = normalize(row_block)
    attn_in = to_half(normed_one * vec_real[0] + vec_real[1])
    projected = jnp.dot(attn_in, qkv_half, preferred_element_type=jnp.float32)
    queries = to_half((projected[:, :D] + vec_real[4]) * HEAD ** (-0.5))
    keys_b = to_half(projected[:, D : 2 * D])
    values_b = to_half(projected[:, 2 * D :] + vec_real[5])
    scores = jnp.einsum(
        "ishd,ithd->ihst",
        heads_split(queries),
        heads_split(keys_b),
        preferred_element_type=jnp.float32,
    )
    log_total = jnp.log(jnp.sum(jnp.exp(scores), axis=-1))
    prob_half = to_half(jnp.exp(scores - log_total[..., None]))
    head_mix = to_half(
        jnp.einsum(
            "ihst,ithd->ishd", prob_half, heads_split(values_b), preferred_element_type=jnp.float32
        ).reshape(-1, D)
    )
    hidden_res = (
        row_block + jnp.dot(head_mix, out_half, preferred_element_type=jnp.float32) + vec_real[6]
    )
    normed_two, inv_two = normalize(hidden_res)
    moe_in = to_half(normed_two * vec_real[2] + vec_real[3])
    exp_logit = jnp.exp(
        jnp.einsum("td,ed->te", moe_in, router_half, preferred_element_type=jnp.float32)
    )
    route_prob = exp_logit / jnp.sum(exp_logit, axis=-1, keepdims=True)
    return (
        attn_in,
        normed_one,
        inv_one,
        queries,
        keys_b,
        values_b,
        log_total,
        head_mix,
        hidden_res,
        normed_two,
        inv_two,
        moe_in,
        route_prob,
    )


def backward_rows(
    saved, grad_moe, cot_rows, grad_gate, ids_here, qkv_half, out_half, vec_real, router_half
):
    (
        attn_in,
        normed_one,
        inv_one,
        queries,
        keys_b,
        values_b,
        log_total,
        head_mix,
        hidden_res,
        normed_two,
        inv_two,
        moe_in,
        route_prob,
    ) = saved
    onehot = expert_table(ids_here)
    grad_prob = jnp.sum(grad_gate[..., None] * onehot, axis=1)
    grad_logit = route_prob * (grad_prob - jnp.sum(route_prob * grad_prob, axis=-1, keepdims=True))
    logit_half = to_half(grad_logit)
    router_grad = jnp.einsum("te,td->ed", logit_half, moe_in, preferred_element_type=jnp.float32)
    grad_moe = grad_moe + jnp.dot(logit_half, router_half, preferred_element_type=jnp.float32)
    gain_two = jnp.sum(grad_moe * normed_two, axis=0)
    shift_two = jnp.sum(grad_moe, axis=0)
    grad_res = cot_rows + normalize_back(grad_moe * vec_real[2], normed_two, inv_two)
    res_half = to_half(grad_res)
    bias_out = jnp.sum(grad_res, axis=0)
    out_part = jnp.einsum("tf,td->fd", head_mix, res_half, preferred_element_type=jnp.float32)
    grad_mix = to_half(
        jnp.einsum("td,fd->tf", res_half, out_half, preferred_element_type=jnp.float32)
    )
    scores = jnp.einsum(
        "ishd,ithd->ihst",
        heads_split(queries),
        heads_split(keys_b),
        preferred_element_type=jnp.float32,
    )
    prob_full = jnp.exp(scores - log_total[..., None])
    prob_half = to_half(prob_full)
    grad_probs = jnp.einsum(
        "ishd,ithd->ihst",
        heads_split(grad_mix),
        heads_split(values_b),
        preferred_element_type=jnp.float32,
    )
    grad_values = jnp.einsum(
        "ihst,ishd->ithd", prob_half, heads_split(grad_mix), preferred_element_type=jnp.float32
    )
    grad_scores = prob_full * (grad_probs - jnp.sum(prob_full * grad_probs, axis=-1, keepdims=True))
    score_half = to_half(grad_scores)
    grad_queries = jnp.einsum(
        "ihst,ithd->ishd", score_half, heads_split(keys_b), preferred_element_type=jnp.float32
    ) * HEAD ** (-0.5)
    grad_keys = jnp.einsum(
        "ihst,ishd->ithd", score_half, heads_split(queries), preferred_element_type=jnp.float32
    )
    grad_queries = grad_queries.reshape(-1, D)
    grad_values = grad_values.reshape(-1, D)
    proj_half = to_half(
        jnp.concatenate([grad_queries, grad_keys.reshape(-1, D), grad_values], axis=1)
    )
    qkv_part = jnp.einsum("td,tq->dq", attn_in, proj_half, preferred_element_type=jnp.float32)
    grad_attn = jnp.einsum("tq,dq->td", proj_half, qkv_half, preferred_element_type=jnp.float32)
    gain_one = jnp.sum(grad_attn * normed_one, axis=0)
    shift_one = jnp.sum(grad_attn, axis=0)
    grad_rows = grad_res + normalize_back(grad_attn * vec_real[0], normed_one, inv_one)
    small_part = jnp.stack(
        [
            gain_one,
            shift_one,
            gain_two,
            shift_two,
            jnp.sum(grad_queries, axis=0),
            jnp.sum(grad_values, axis=0),
            bias_out,
        ]
    )
    return (grad_rows, qkv_part, out_part, small_part, router_grad)


def adamw_step(weight, grad, first_m, second_m):
    new_first = BETA_ONE * first_m + (1.0 - BETA_ONE) * grad
    new_second = BETA_TWO * second_m + (1.0 - BETA_TWO) * grad * grad
    step_dir = new_first / CORR_ONE / (jnp.sqrt(new_second / CORR_TWO) + ADAM_EPS)
    return (weight - LEARN_RATE * (step_dir + WEIGHT_DECAY * weight), new_first, new_second)


def body(
    tokens,
    cotangent,
    expert_ids,
    slot_pos,
    qkv_w,
    qkv_m,
    qkv_v,
    out_w,
    out_m,
    out_v,
    vectors,
    vec_m,
    vec_v,
    w_in,
    w_in_m,
    w_in_v,
    w_out,
    w_out_m,
    w_out_v,
    b_in,
    b_in_m,
    b_in_v,
):
    qkv_shard = to_half(qkv_w)
    out_shard = to_half(out_w)
    vec_shard = to_half(vectors)
    qkv_half, out_half, vec_half = (
        lax.all_gather(qkv_shard, ("dp", "group"), axis=0, tiled=True),
        lax.all_gather(out_shard, ("dp", "group"), axis=0, tiled=True),
        lax.all_gather(vec_shard, ("dp", "group"), axis=1, tiled=True),
    )
    win_full, wout_full, bin_full = (
        lax.all_gather(to_half(w_in), "group", axis=0, tiled=True),
        lax.all_gather(to_half(w_out), "group", axis=1, tiled=True),
        lax.all_gather(to_half(b_in), "group", axis=0, tiled=True),
    )
    vec_real = vec_half.astype(jnp.float32)
    router_half = vec_half[7 : 7 + EXPERTS]
    out_bias = vec_real[7 + EXPERTS :]
    hid_cols = win_full.shape[1]
    local_exp = max(1, hid_cols // FF)
    hid_width = hid_cols // local_exp
    split_count = FF // hid_width
    dp_count = lax.axis_size("dp")
    weight_in = win_full.reshape(D, local_exp, hid_width).transpose(1, 0, 2)
    weight_out = wout_full.reshape(local_exp, hid_width, D)
    bias_in = bin_full.astype(jnp.float32).reshape(local_exp, hid_width)

    def spread(buffer):
        return jnp.repeat(buffer.reshape(EXPERTS, CAP, D), split_count, axis=0)

    def to_experts(arrived):
        return (
            arrived.reshape(dp_count, local_exp, CAP, D)
            .transpose(1, 0, 2, 3)
            .reshape(local_exp, dp_count * CAP, D)
        )

    def to_sources(expert_rows):
        return (
            expert_rows.reshape(local_exp, dp_count, CAP, D)
            .transpose(1, 0, 2, 3)
            .reshape(dp_count * local_exp, CAP, D)
        )

    def join_parts(arrived):
        return jnp.sum(arrived.reshape(EXPERTS, split_count, CAP, D), axis=1).reshape(
            EXPERTS * CAP, D
        )

    saved = forward_rows(tokens, qkv_half, out_half, vec_real, router_half)
    slot_hits, kept_mask = slot_table(expert_ids, slot_pos)
    packed = to_half(
        jnp.einsum(
            "ts,td->sd",
            to_half(jnp.sum(slot_hits, axis=1)),
            saved[11],
            preferred_element_type=jnp.float32,
        )
    )
    routed_rows = to_experts(
        lax.all_to_all(spread(packed), "dp", split_axis=0, concat_axis=0, tiled=True)
    )
    pre_act = (
        jnp.einsum("erd,edh->erh", routed_rows, weight_in, preferred_element_type=jnp.float32)
        + bias_in[:, None, :]
    )
    expert_res = jnp.einsum(
        "erh,ehd->erd",
        to_half(jax.nn.gelu(pre_act)),
        weight_out,
        preferred_element_type=jnp.float32,
    )
    combined = join_parts(
        lax.all_to_all(
            to_sources(expert_res).astype(jnp.bfloat16),
            "dp",
            split_axis=0,
            concat_axis=0,
            tiled=True,
        ).astype(jnp.float32)
    )
    chosen, kept_mask = select_rows(combined, expert_ids, slot_pos)
    onehot = expert_table(expert_ids)
    chosen = chosen + jnp.einsum("tke,ed->tkd", onehot, out_bias, precision=EXACT)
    gate_vals = jnp.where(kept_mask, jnp.take_along_axis(saved[12], expert_ids, axis=1), 0.0)
    block_out = saved[8] + jnp.sum(gate_vals[..., None] * chosen, axis=1)
    grad_gate = jnp.where(kept_mask, jnp.sum(cotangent[:, None, :] * chosen, axis=-1), 0.0)
    weighted = gate_vals[..., None] * cotangent[:, None, :]
    grad_packed = to_half(jnp.einsum("tks,tkd->sd", slot_hits, weighted, precision=EXACT))
    bias_grad = jnp.einsum("tke,tkd->ed", onehot, weighted, precision=EXACT)
    grad_routed = to_experts(
        lax.all_to_all(spread(grad_packed), "dp", split_axis=0, concat_axis=0, tiled=True)
    )
    activated, gelu_back = jax.vjp(jax.nn.gelu, pre_act)
    act_half = to_half(activated)
    grad_act = jnp.einsum(
        "erd,ehd->erh", grad_routed, weight_out, preferred_element_type=jnp.float32
    )
    grad_wout = jnp.einsum(
        "erh,erd->ehd", act_half, grad_routed, preferred_element_type=jnp.float32
    )
    grad_pre = gelu_back(grad_act)[0]
    grad_bias_in = jnp.sum(grad_pre, axis=1)
    pre_half = to_half(grad_pre)
    grad_win = jnp.einsum("erd,erh->edh", routed_rows, pre_half, preferred_element_type=jnp.float32)
    grad_inputs = jnp.einsum(
        "erh,edh->erd", pre_half, weight_in, preferred_element_type=jnp.float32
    )
    slot_grads = join_parts(
        lax.all_to_all(
            to_sources(grad_inputs).astype(jnp.bfloat16),
            "dp",
            split_axis=0,
            concat_axis=0,
            tiled=True,
        ).astype(jnp.float32)
    )
    w_in_grad, w_out_grad, b_in_grad = (
        lax.psum_scatter(
            grad_win.transpose(1, 0, 2).reshape(D, hid_cols).astype(jnp.bfloat16),
            "group",
            scatter_dimension=0,
            tiled=True,
        ).astype(jnp.float32),
        lax.psum_scatter(
            grad_wout.reshape(hid_cols, D).astype(jnp.bfloat16),
            "group",
            scatter_dimension=1,
            tiled=True,
        ).astype(jnp.float32),
        lax.psum_scatter(
            grad_bias_in.reshape(hid_cols).astype(jnp.bfloat16),
            "group",
            scatter_dimension=0,
            tiled=True,
        ).astype(jnp.float32),
    )
    picked, kept_mask = select_rows(slot_grads, expert_ids, slot_pos)
    grad_moe = jnp.sum(jnp.where(kept_mask[..., None], picked, 0.0), axis=1)
    input_grad, qkv_part, out_part, small_part, router_grad = backward_rows(
        saved, grad_moe, cotangent, grad_gate, expert_ids, qkv_half, out_half, vec_real, router_half
    )
    vec_part = jnp.concatenate([small_part, router_grad, bias_grad], axis=0)
    qkv_grad, out_grad, vec_grad = (
        lax.psum_scatter(qkv_part, ("dp", "group"), scatter_dimension=0, tiled=True),
        lax.psum_scatter(out_part, ("dp", "group"), scatter_dimension=0, tiled=True),
        lax.psum_scatter(vec_part, ("dp", "group"), scatter_dimension=1, tiled=True),
    )
    branch_bias_grad = jnp.concatenate([vec_grad[6:7], vec_grad[7 + EXPERTS :]], axis=0)
    qkv_new, qkv_m_new, qkv_v_new = adamw_step(qkv_w, qkv_grad, qkv_m, qkv_v)
    out_new, out_m_new, out_v_new = adamw_step(out_w, out_grad, out_m, out_v)
    vec_new, vec_m_new, vec_v_new = adamw_step(vectors, vec_grad, vec_m, vec_v)
    w_in_new, w_in_m_new, w_in_v_new = adamw_step(w_in, w_in_grad, w_in_m, w_in_v)
    w_out_new, w_out_m_new, w_out_v_new = adamw_step(w_out, w_out_grad, w_out_m, w_out_v)
    b_in_new, b_in_m_new, b_in_v_new = adamw_step(b_in, b_in_grad, b_in_m, b_in_v)
    return (
        block_out,
        input_grad,
        qkv_grad,
        qkv_new,
        qkv_m_new,
        qkv_v_new,
        out_grad,
        out_new,
        out_m_new,
        out_v_new,
        vec_grad,
        vec_new,
        vec_m_new,
        vec_v_new,
        w_in_grad,
        w_in_new,
        w_in_m_new,
        w_in_v_new,
        w_out_grad,
        w_out_new,
        w_out_m_new,
        w_out_v_new,
        b_in_grad,
        b_in_new,
        b_in_m_new,
        b_in_v_new,
        branch_bias_grad,
    )


def solution(mesh):
    return jax.shard_map(
        body,
        mesh=mesh,
        in_specs=(
            P(("dp", "group"), None),
            P(("dp", "group"), None),
            P(("dp", "group"), None),
            P(("dp", "group"), None),
            P(("dp", "group"), None),
            P(("dp", "group"), None),
            P(("dp", "group"), None),
            P(("dp", "group"), None),
            P(("dp", "group"), None),
            P(("dp", "group"), None),
            P(None, ("dp", "group")),
            P(None, ("dp", "group")),
            P(None, ("dp", "group")),
            P("group", "dp"),
            P("group", "dp"),
            P("group", "dp"),
            P("dp", "group"),
            P("dp", "group"),
            P("dp", "group"),
            P(("dp", "group")),
            P(("dp", "group")),
            P(("dp", "group")),
        ),
        out_specs=(
            P(("dp", "group"), None),
            P(("dp", "group"), None),
            P(("dp", "group"), None),
            P(("dp", "group"), None),
            P(("dp", "group"), None),
            P(("dp", "group"), None),
            P(("dp", "group"), None),
            P(("dp", "group"), None),
            P(("dp", "group"), None),
            P(("dp", "group"), None),
            P(None, ("dp", "group")),
            P(None, ("dp", "group")),
            P(None, ("dp", "group")),
            P(None, ("dp", "group")),
            P("group", "dp"),
            P("group", "dp"),
            P("group", "dp"),
            P("group", "dp"),
            P("dp", "group"),
            P("dp", "group"),
            P("dp", "group"),
            P("dp", "group"),
            P(("dp", "group")),
            P(("dp", "group")),
            P(("dp", "group")),
            P(("dp", "group")),
            P(None, ("dp", "group")),
        ),
        check_vma=False,
    )
```

profile of v0, /device:TPU:0, one launch (start us, length us, event | category | flops | bytes accessed | tf_op | source)
XLA Modules:
  0.0 1328.5 jit_solution(7883423809906446272)
XLA Ops:
  7.2 1.6 convert_element_type.146
  8.9 1.5 convert_element_type.154
  10.5 4.1 convert_element_type.159
  14.7 71.7 %all_gather.18 = bf16[39,768]{0,1:T(8,128)(2,1)S(1)} all-gather(bf16[39,24]{0,1:T(8,128)(2,1)S(1)} %convert_element_type.143), channel_id=1, replica_groups=mesh['dp'=8,'group'=4] {'dp','group'}, dimensions={1}, use_global_device_ids=true | all-gather | bytes 61776 | tf_op jit(solution)/shard_map/all_gather | solution.py:233
  87.0 1.4 slice_reduce_fusion.1
  88.5 3.0 fusion.87
  94.4 1.3 copy.234
  95.7 2.0 fusion.102
  97.7 3.3 convolution_convert_fusion.4
  101.0 30.0 %all-gather.8.cloned.1.call-done = bf16[768,768]{1,0:T(8,128)(2,1)} async-done(((bf16[24,768]{1,0:T(8,128)(2,1)}), bf16[768,768]{1,0:T(8,128)(2,1)}) %all-gather.8.cloned.1.call-update) | async-done | bytes 1179664 | tf_op jit(solution)/shard_map/all_gather | solution.py:232
  131.0 1.8 fusion.97
  133.8 6.0 gather_fusion
  140.1 1.5 fusion.24
  142.6 4.2 all-to-all-start.2
  148.5 11.0 all-to-all-done.2
  159.5 4.2 all-to-all-start
  163.8 15.5 %all-gather = bf16[4,1,1536]{2,1,0:T(2,128)(2,1)S(1)} all-gather(bf16[1,1,1536]{2,1,0:T(2,128)(2,1)S(1)} %reshape.315), channel_id=1, replica_groups=mesh['dp'=8,'group'=4] {'group'}, dimensions={0}, use_global_device_ids=true | all-gather | bytes 15360 | tf_op jit(solution)/shard_map/all_gather | solution.py:238
  179.4 2.6 copy.253
  182.0 1.8 copy.240
  183.8 115.5 %all-gather.10.cloned.1.call-done = bf16[768,6144]{1,0:T(8,128)(2,1)} async-done(((bf16[192,6144]{1,0:T(8,128)(2,1)}), bf16[768,6144]{1,0:T(8,128)(2,1)}) %all-gather.10.cloned.1.call-update) | async-done | bytes 9437200 | tf_op jit(solution)/shard_map/all_gather | solution.py:236
  299.3 12.7 copy.241
  312.0 12.7 copy.242
  324.7 5.8 fusion.3
  330.5 6.4 convolution_convert_fusion
  336.9 12.7 copy.270
  350.0 159.4 %reduce-scatter.12.cloned.1.call-done = bf16[6144,192]{0,1:T(8,128)(2,1)} async-done(((bf16[6144,768]{0,1:T(8,128)(2,1)}), bf16[6144,192]{0,1:T(8,128)(2,1)}) %reduce-scatter.12.cloned.1.call-update) | async-done | bytes 2359312 | tf_op jit(solution)/shard_map/reduce_scatter | solution.py:349
  509.3 14.4 %multiply_subtract_fusion = (f32[6144,192]{0,1:T(8,128)}, f32[6144,192]{0,1:T(8,128)}, f32[6144,192]{0,1:T(8,128)}, f32[6144,192]{0,1:T(8,128)}, bf16[6144,192]{0,1:T(8,128)(2,1)}) fusion(f32[6144,192]{0,1:T(8,128)} %param.40, f32[6144,192]{0,1:T(8,128)} %param.41, f32[6144,192]{0,1:T(8,128)} %param.42, bf16[6144,192]{0,1:T(8,128)(2,1)} %reduce-scatter.12.cloned.1.call-done), kind=kLoop, calls=%fused_computation.23 | loop fusion | flops 20054016 | bytes 37748736 | tf_op jit(solution)/shard_map/sub | solution.py:200
  525.7 165.9 %all-gather.12.cloned.1.call-done = bf16[6144,768]{0,1:T(8,128)(2,1)} async-done(((bf16[6144,192]{0,1:T(8,128)(2,1)}), bf16[6144,768]{0,1:T(8,128)(2,1)}) %all-gather.12.cloned.1.call-update) | async-done | bytes 9437200 | tf_op jit(solution)/shard_map/all_gather | solution.py:237
  691.6 12.8 copy.244
  704.4 7.9 convolution_convert_fusion.1
  713.5 6.8 fusion.101
  721.8 4.1 all-to-all-start.1
  726.0 7.6 fusion.27
  735.1 3.5 all-to-all-done.1
  738.6 4.2 all-to-all-start.3
  742.8 1.3 reshape.281
  744.2 2.5 gather_fusion.1
  746.7 2.1 reshape.322
  748.8 2.7 multiply_reduce_fusion.1
  751.7 3.7 all-to-all-done.3
  755.4 1.3 reshape.283
  756.7 2.5 gather_fusion.2
  759.2 2.9 reshape.326
  762.1 7.5 fusion.34
  770.8 2.7 fusion.92
  775.0 1.6 fusion.103
  776.7 3.8 multiply_reduce_fusion
  780.4 2.1 multiply_convert_fusion.1
  783.6 4.1 fusion.95
  787.7 4.2 multiply_reduce_fusion.4
  794.0 4.2 concatenate.11
  798.3 1.9 fusion.74
  800.3 4.2 fusion.56
  805.6 6.8 convert_bitcast_fusion
  812.4 12.7 copy.267
  825.1 12.7 copy.280
  839.7 16.2 %all-reduce.1 = bf16[6144]{0:T(1024)(128)(2,1)S(1)} all-reduce(bf16[6144]{0:T(1024)(128)(2,1)S(1)} %bitcast.139), channel_id=7, replica_groups=mesh['dp'=8,'group'=4] {'group'}, use_global_device_ids=true, to_apply=%region_30.32.clone | all-reduce | flops 6144 | bytes 24576
  857.7 58.3 %all-reduce.4.cloned.1.call-done = f32[39,768]{1,0:T(8,128)} async-done(((f32[39,768]{1,0:T(8,128)}), f32[39,768]{1,0:T(8,128)}) %all-reduce.4.cloned.1.call-update) | async-done | bytes 119824
  919.8 101.8 %reduce-scatter.10.cloned.1.call-done = f32[24,768]{1,0:T(8,128)} async-done(((f32[768,768]{1,0:T(8,128)}), f32[24,768]{1,0:T(8,128)}) %reduce-scatter.10.cloned.1.call-update) | async-done | bytes 73744 | tf_op jit(solution)/shard_map/reduce_scatter | solution.py:370
  1021.6 1.6 multiply_subtract_fusion.3
  1023.2 123.9 %reduce-scatter.8.cloned.1.call-done = f32[24,2304]{1,0:T(8,128)} async-done(((f32[768,2304]{1,0:T(8,128)}), f32[24,2304]{1,0:T(8,128)}) %reduce-scatter.8.cloned.1.call-update) | async-done | bytes 221200 | tf_op jit(solution)/shard_map/reduce_scatter | solution.py:369
  1147.1 1.9 multiply_subtract_fusion.2
  1149.0 161.0 %reduce-scatter.14.cloned.1.call-done = bf16[192,6144]{1,0:T(8,128)(2,1)} async-done(((bf16[768,6144]{1,0:T(8,128)(2,1)}), bf16[192,6144]{1,0:T(8,128)(2,1)}) %reduce-scatter.14.cloned.1.call-update) | async-done | bytes 2359312 | tf_op jit(solution)/shard_map/reduce_scatter | solution.py:343
  1310.0 11.7 multiply_subtract_fusion.1
  (214 shorter events, 27.9 us)
Async XLA Ops:
  7.2 81.3 %all-gather.6.cloned.1.call-start = ((), (), s32[]{:S(2)}) async-start(), calls=%async_computation.8 | async-start | bytes 3649536 | tf_op jit(solution)/shard_map/all_gather | solution.py:231
  8.9 122.1 %all-gather.8.cloned.1.call-start = ((), (), s32[]{:S(2)}) async-start(), calls=%async_computation.9 | async-start | bytes 1216512 | tf_op jit(solution)/shard_map/all_gather | solution.py:232
  10.5 75.9 %copy-start.29 = (s32[197,2]{0,1:T(2,128)S(1)}, s32[197,2]{0,1:T(2,128)}, u32[]{:S(2)}) copy-start(s32[197,2]{0,1:T(2,128)} %param.26) | copy-start | bytes 4732
  10.5 76.2 %copy-start = (f32[197,768]{1,0:T(8,128)S(1)}, f32[197,768]{1,0:T(8,128)}, u32[]{:S(2)}) copy-start(f32[197,768]{1,0:T(8,128)} %param.24) | copy-start | bytes 1815556
  10.5 288.8 %all-gather.10.cloned.1.call-start = ((), (), s32[]{:S(2)}) async-start(), calls=%async_computation.10 | async-start | bytes 11796480 | tf_op jit(solution)/shard_map/all_gather | solution.py:236
  86.4 46.9 %copy-start.13 = (bf16[39,768]{0,1:T(8,128)(2,1)}, bf16[39,768]{0,1:T(8,128)(2,1)S(1)}, u32[]{:S(2)}) copy-start(bf16[39,768]{0,1:T(8,128)(2,1)S(1)} %all_gather.18) | copy-start | bytes 179716
  88.5 5.9 copy-start.37
  94.4 38.4 %copy-start.4 = (bf16[197,768]{0,1:T(8,128)(2,1)}, bf16[197,768]{0,1:T(8,128)(2,1)S(1)}, u32[]{:S(2)}) copy-start(bf16[197,768]{0,1:T(8,128)(2,1)S(1)} %copy.236) | copy-start | bytes 907780
  95.7 37.4 %copy-start.19 = (bf16[197,768]{0,1:T(8,128)(2,1)}, bf16[197,768]{0,1:T(8,128)(2,1)S(1)}, u32[]{:S(2)}) copy-start(bf16[197,768]{0,1:T(8,128)(2,1)S(1)} %copy.234) | copy-start | bytes 907780
  101.0 38.7 %copy-start.17 = (bf16[12,64,197]{2,1,0:T(8,128)(2,1)}, bf16[12,64,197]{2,1,0:T(8,128)(2,1)S(1)}, u32[]{:S(2)}) copy-start(bf16[12,64,197]{2,1,0:T(8,128)(2,1)S(1)} %convolution_convert_fusion.4) | copy-start | bytes 907780
  133.1 6.7 copy-start.41
  133.3 13.8 %copy-start.11 = (bf16[197,768]{1,0:T(8,128)(2,1)}, bf16[197,768]{1,0:T(8,128)(2,1)S(1)}, u32[]{:S(2)}) copy-start(bf16[197,768]{1,0:T(8,128)(2,1)S(1)} %add_convert_fusion) | copy-start | bytes 907780
  133.7 6.0 copy-start.45
  133.7 6.3 copy-start.55
  133.7 6.3 copy-start.9
  139.8 24.0 %copy-start.33 = (f32[1536]{0:T(1024)S(1)}, f32[1536]{0:T(1024)}, u32[]{:S(2)}) copy-start(f32[1536]{0:T(1024)} %param.43) | copy-start | bytes 18436
  140.0 383.8 %copy-start.35 = (pred[197,2]{0,1:T(4,128)(4,1)}, pred[197,2]{0,1:T(4,128)(4,1)S(1)}, u32[]{:S(2)}) copy-start(pred[197,2]{0,1:T(4,128)(4,1)S(1)} %get-tuple-element.204) | copy-start | bytes 1186
  140.0 384.4 %copy-start.39 = (f32[197,2]{0,1:T(2,128)}, f32[197,2]{0,1:T(2,128)S(1)}, u32[]{:S(2)}) copy-start(f32[197,2]{0,1:T(2,128)S(1)} %get-tuple-element.203) | copy-start | bytes 4732
  140.1 384.2 %copy-start.51 = (pred[197,2]{0,1:T(4,128)(4,1)}, pred[197,2]{0,1:T(4,128)(4,1)S(1)}, u32[]{:S(2)}) copy-start(pred[197,2]{0,1:T(4,128)(4,1)S(1)} %get-tuple-element.205) | copy-start | bytes 1186
  142.6 16.9 %all-to-all-start.2 = ((bf16[16,25,768]{2,1,0:T(8,128)(2,1)}), bf16[16,25,768]{2,1,0:T(8,128)(2,1)}, u32[]{:S(2)}, u32[]{:S(2)}) async-start(bf16[16,25,768]{2,1,0:T(8,128)(2,1)} %reshape_broadcast_in_dim_reshape.7), calls=%async_computation.2 | async-start | bytes 1572864 | tf_op jit(solution)/shard_map/all_to_all | solution.py:316
  159.5 22.5 %all-to-all-start = ((bf16[16,25,768]{2,1,0:T(8,128)(2,1)}), bf16[16,25,768]{2,1,0:T(8,128)(2,1)}, u32[]{:S(2)}, u32[]{:S(2)}) async-start(bf16[16,25,768]{2,1,0:T(8,128)(2,1)} %reshape_broadcast_in_dim_reshape.6), calls=%async_computation | async-start | bytes 1572864 | tf_op jit(solution)/shard_map/all_to_all | solution.py:285
  163.7 345.7 %reduce-scatter.12.cloned.1.call-start = ((), (), s32[]{:S(2)}) async-start(), calls=%async_computation.14 | async-start | bytes 11796480 | tf_op jit(solution)/shard_map/reduce_scatter | solution.py:349
  183.8 140.9 %copy-start.6 = (bf16[8,2,25,768]{3,1,2,0:T(2,128)(2,1)}, bf16[8,2,25,768]{3,1,2,0:T(2,128)(2,1)S(1)}, u32[]{:S(2)}) copy-start(bf16[8,2,25,768]{3,1,2,0:T(2,128)(2,1)S(1)} %copy.240) | copy-start | bytes 1843204
  324.7 5.9 copy-start.21
  330.5 6.4 copy-start.1
  349.7 341.9 %all-gather.12.cloned.1.call-start = ((), (), s32[]{:S(2)}) async-start(), calls=%async_computation.11 | async-start | bytes 11796480 | tf_op jit(solution)/shard_map/all_gather | solution.py:237
  691.6 20.7 %slice-start = ((s8[4915200]{0:T(1024)(128)(4,1)}), s8[720896]{0:T(1024)(128)(4,1)S(1)}, s32[]{:S(2)}) async-start(s8[4915200]{0:T(1024)(128)(4,1)} %bitcast.109), calls=%async_computation.17 | async-start | bytes 1441792
  704.4 7.9 slice-start.1
  704.4 9.1 copy-start.8
  704.4 9.2 copy-start.22
  721.8 16.7 %all-to-all-start.1 = ((bf16[16,25,768]{2,1,0:T(8,128)(2,1)}), bf16[16,25,768]{2,1,0:T(8,128)(2,1)S(1)}, u32[]{:S(2)}, u32[]{:S(2)}) async-start(bf16[16,25,768]{2,1,0:T(8,128)(2,1)} %bitcast.122), calls=%async_computation.1 | async-start | bytes 1572864 | tf_op jit(solution)/shard_map/all_to_all | solution.py:298
  738.6 16.8 %all-to-all-start.3 = ((bf16[16,25,768]{2,1,0:T(8,128)(2,1)}), bf16[16,25,768]{2,1,0:T(8,128)(2,1)}, u32[]{:S(2)}, u32[]{:S(2)}) async-start(bf16[16,25,768]{2,1,0:T(8,128)(2,1)} %bitcast.23), calls=%async_computation.3 | async-start | bytes 1572864 | tf_op jit(solution)/shard_map/all_to_all | solution.py:334
  742.8 173.2 %all-reduce.4.cloned.1.call-start = ((), (), s32[]{:S(2)}) async-start(), calls=%async_computation.16 | async-start | bytes 245760
  746.7 4.8 copy-start.36
  746.7 4.8 copy-start.46
  746.7 4.9 copy-start.12
  756.7 13.0 copy-start.42
  759.2 11.6 copy-start.10
  762.1 11.4 copy-start.15
  782.6 5.1 copy-start.38
  787.7 6.2 copy-start.47
  787.7 6.2 copy-start.44
  787.7 6.3 copy-start.43
  787.7 6.3 copy-start.26
  787.7 10.6 copy-start.3
  787.7 10.6 copy-start.18
  798.2 223.4 %reduce-scatter.10.cloned.1.call-start = ((), (), s32[]{:S(2)}) async-start(), calls=%async_computation.13 | async-start | bytes 2433024 | tf_op jit(solution)/shard_map/reduce_scatter | solution.py:370
  800.2 346.9 %reduce-scatter.8.cloned.1.call-start = ((), (), s32[]{:S(2)}) async-start(), calls=%async_computation.12 | async-start | bytes 7299072 | tf_op jit(solution)/shard_map/reduce_scatter | solution.py:369
  804.5 505.5 %reduce-scatter.14.cloned.1.call-start = ((), (), s32[]{:S(2)}) async-start(), calls=%async_computation.15 | async-start | bytes 11796480 | tf_op jit(solution)/shard_map/reduce_scatter | solution.py:343
  837.8 18.1 %copy-start.34 = (f32[1536]{0:T(1024)S(1)}, f32[1536]{0:T(1024)}, u32[]{:S(2)}) copy-start(f32[1536]{0:T(1024)} %param.43) | copy-start | bytes 18436
  837.8 18.1 %copy-start.53 = (f32[1536]{0:T(1024)S(1)}, f32[1536]{0:T(1024)}, u32[]{:S(2)}) copy-start(f32[1536]{0:T(1024)} %param.44) | copy-start | bytes 18436
  837.8 18.1 %copy-start.54 = (f32[1536]{0:T(1024)S(1)}, f32[1536]{0:T(1024)}, u32[]{:S(2)}) copy-start(f32[1536]{0:T(1024)} %param.45) | copy-start | bytes 18436
  837.8 18.8 %copy-start.57 = (f32[197]{0:T(256)S(1)}, f32[197]{0:T(256)}, u32[]{:S(2)}) copy-start(f32[197]{0:T(256)} %get-tuple-element.166) | copy-start | bytes 2368
  837.8 18.8 %copy-start.56 = (f32[197]{0:T(256)S(1)}, f32[197]{0:T(256)}, u32[]{:S(2)}) copy-start(f32[197]{0:T(256)} %get-tuple-element.169) | copy-start | bytes 2368
  837.9 81.3 %copy-start.31 = (f32[39,24]{0,1:T(8,128)S(1)}, f32[39,24]{0,1:T(8,128)}, u32[]{:S(2)}) copy-start(f32[39,24]{0,1:T(8,128)} %param.34) | copy-start | bytes 11236
  837.9 81.3 %copy-start.49 = (f32[39,24]{0,1:T(8,128)S(1)}, f32[39,24]{0,1:T(8,128)}, u32[]{:S(2)}) copy-start(f32[39,24]{0,1:T(8,128)} %param.35) | copy-start | bytes 11236
  837.9 81.3 %copy-start.50 = (f32[39,24]{0,1:T(8,128)S(1)}, f32[39,24]{0,1:T(8,128)}, u32[]{:S(2)}) copy-start(f32[39,24]{0,1:T(8,128)} %param.36) | copy-start | bytes 11236
  837.9 183.7 %copy-start.23 = (f32[24,768]{1,0:T(8,128)S(1)}, f32[24,768]{1,0:T(8,128)}, u32[]{:S(2)}) copy-start(f32[24,768]{1,0:T(8,128)} %param.31) | copy-start | bytes 221188
  837.9 183.7 %copy-start.27 = (f32[24,768]{1,0:T(8,128)S(1)}, f32[24,768]{1,0:T(8,128)}, u32[]{:S(2)}) copy-start(f32[24,768]{1,0:T(8,128)} %param.32) | copy-start | bytes 221188
  837.9 183.7 %copy-start.28 = (f32[24,768]{1,0:T(8,128)S(1)}, f32[24,768]{1,0:T(8,128)}, u32[]{:S(2)}) copy-start(f32[24,768]{1,0:T(8,128)} %param.33) | copy-start | bytes 221188
  837.9 309.2 %copy-start.20 = (f32[24,2304]{1,0:T(8,128)S(1)}, f32[24,2304]{1,0:T(8,128)}, u32[]{:S(2)}) copy-start(f32[24,2304]{1,0:T(8,128)} %param.28) | copy-start | bytes 663556
  837.9 309.2 %copy-start.24 = (f32[24,2304]{1,0:T(8,128)S(1)}, f32[24,2304]{1,0:T(8,128)}, u32[]{:S(2)}) copy-start(f32[24,2304]{1,0:T(8,128)} %param.29) | copy-start | bytes 663556
  838.0 309.2 %copy-start.25 = (f32[24,2304]{1,0:T(8,128)S(1)}, f32[24,2304]{1,0:T(8,128)}, u32[]{:S(2)}) copy-start(f32[24,2304]{1,0:T(8,128)} %param.30) | copy-start | bytes 663556
  916.9 404.8 %copy-start.32 = (f32[39,24]{0,1:T(8,128)}, f32[39,24]{0,1:T(8,128)S(1)}, u32[]{:S(2)}) copy-start(f32[39,24]{0,1:T(8,128)S(1)} %copy.271) | copy-start | bytes 11236
  (10 other events, 29.4 us)
Sparse Core Ops, SparseCore 0:
  11.4 63.3 all-gather.5
  78.2 52.7 all-gather.7
  133.2 166.0 all-gather.9
  349.8 159.5 reduce-scatter.11
  523.9 167.6 all-gather.11
  798.4 117.6 all-reduce.3
  922.4 99.1 reduce-scatter.9
  1028.8 118.2 reduce-scatter.7
  1149.5 160.4 reduce-scatter.13
where the time goes:
time: 1340 us; the launch traced here: 1330 us
  waiting for transfers between devices  934 us (70%)
  local copies, waits for them, and re-layouts  123 us (9%)
  blocking collectives  103 us (8%)
  matrix products  80.3 us (6%)
  other arithmetic  54.2 us (4%)
  starting transfers between devices  17.4 us (1%)
  between operations  15.7 us (1%)
    all_gather x1, waiting for transfers between devices, body(): lax.all_gather(to_half(w_out), 'group', axis=1, tiled=True)  166 us
    reduce_scatter x1, waiting for transfers between devices, body(): lax.psum_scatter(grad_win.transpose(1, 0, 2).reshape(D, hid_cols).astype(...  161 us
    reduce_scatter x1, waiting for transfers between devices, body(): lax.psum_scatter(grad_wout.reshape(hid_cols, D).astype(jnp.bfloat16), 'gr...  159 us
    reduce_scatter x1, waiting for transfers between devices, body(): lax.psum_scatter(qkv_part, ('dp', 'group'), scatter_dimension=0, tiled=True)  124 us
    all_gather x1, waiting for transfers between devices, body(): lax.all_gather(to_half(w_in), 'group', axis=0, tiled=True)  115 us
    reduce_scatter x1, waiting for transfers between devices, body(): lax.psum_scatter(out_part, ('dp', 'group'), scatter_dimension=0, tiled=True)  102 us
    all_gather x1, blocking collectives, body(): lax.all_gather(vec_shard, ('dp', 'group'), axis=1, tiled=True)  71.7 us
    unnamed x10, waiting for transfers between devices  58.4 us
  transfers between devices with their start and end apart: 13, of which 11 were waited for; matrix products, arithmetic and copies ran while one was open for 8% of the time, Pallas kernels for 0%

commit v1 on v0

--- a/solution.py
+++ b/solution.py
@@ -1,7 +1,7 @@
 import jax
 import jax.numpy as jnp
 from jax import lax
-from jax.sharding import PartitionSpec as P
+from jax.sharding import Mesh, PartitionSpec as P
 
 D = 768
 HEADS = 12
@@ -200,7 +200,7 @@
     return (weight - LEARN_RATE * (step_dir + WEIGHT_DECAY * weight), new_first, new_second)
 
 
-def body(
+def body_any(
     tokens,
     cotangent,
     expert_ids,
@@ -408,62 +408,429 @@
     )
 
 
+AXES = ("y", "x", "core", "group")
+CHIPS = ("y", "x", "group")
+COLUMN = ("core", "group")
+SWAP = [(0, 1), (1, 0)]
+WIDE = 3200
+SHARD = 24
+
+
+def exact_dot(left, right, dims):
+    return lax.dot_general(left, right, (dims, ((), ())), preferred_element_type=jnp.float32)
+
+
+def shift_perm(step):
+    return [(i, (i + step) % 4) for i in range(4)]
+
+
+def place():
+    return tuple(lax.axis_index(name) for name in AXES)
+
+
+def join_swap(rows, axis_name):
+    return jnp.concatenate([rows, lax.ppermute(rows, axis_name, SWAP)], axis=0)
+
+
+def gather_line(shard):
+    return [shard] + [lax.ppermute(shard, "group", shift_perm(step)) for step in (1, 2, 3)]
+
+
+def gather_plane(blocks):
+    first = jnp.concatenate(blocks[:2], axis=0)
+    second = jnp.concatenate(blocks[2:], axis=0)
+    first, second = join_swap(first, "x"), join_swap(second, "y")
+    first, second = join_swap(first, "y"), join_swap(second, "x")
+    return jnp.concatenate([join_swap(first, "core"), join_swap(second, "core")], axis=0)
+
+
+def fold_swap(rows, axis_name):
+    half = rows.shape[0] // 2
+    arrived = lax.ppermute(rows[half:], axis_name, SWAP)
+    return to_half(rows[:half].astype(jnp.float32) + arrived.astype(jnp.float32))
+
+
+def scatter_sum(rows):
+    half = rows.shape[0] // 2
+    first, second = fold_swap(rows[:half], "core"), fold_swap(rows[half:], "core")
+    first, second = fold_swap(first, "y"), fold_swap(second, "x")
+    first, second = fold_swap(first, "x"), fold_swap(second, "y")
+    blocks = [first[:SHARD], first[SHARD:], second[:SHARD], second[SHARD:]]
+    total = blocks[0].astype(jnp.float32)
+    for step in (1, 2, 3):
+        total = total + lax.ppermute(blocks[step], "group", shift_perm(-step)).astype(jnp.float32)
+    return total
+
+
+def row_order():
+    row_y, row_x, core, line = place()
+    spot = jnp.arange(D)
+    half = spot // 384
+    other = (spot // 192) % 2
+    outer = (spot // 96) % 2
+    inner = (spot // 48) % 2
+    step = half * 2 + (spot // SHARD) % 2
+    y_rel = jnp.where(half == 0, outer, inner)
+    x_rel = jnp.where(half == 0, inner, outer)
+    owner = (((row_y ^ y_rel) * 2 + (row_x ^ x_rel)) * 2 + (core ^ other)) * 4 + (line - step) % 4
+    feature = owner * SHARD + spot % SHARD
+    return to_half(feature[:, None] == jnp.arange(D)[None, :])
+
+
+def column_pairs(turn):
+    pairs = []
+    for core in range(2):
+        for line in range(4):
+            part = (line + turn) % 4
+            pairs.append((core * 4 + line, (part % 2) * 4 + 2 * core + part // 2))
+    return pairs
+
+
+def to_hosts(rows):
+    row_y, row_x, core, line = place()
+    parts = rows.reshape(rows.shape[0], 4, -1)
+    arrived = []
+    for turn in range(4):
+        part = lax.dynamic_index_in_dim(parts, (line + turn) % 4, axis=1, keepdims=False)
+        arrived.append(lax.ppermute(to_half(part), COLUMN, column_pairs(turn)))
+    return arrived
+
+
+def settle(arrived):
+    row_y, row_x, core, line = place()
+    stacked = jnp.stack(arrived, axis=0)
+    here = 2 * (line % 2) + core
+    pieces = [
+        lax.dynamic_index_in_dim(stacked, (here - piece) % 4, axis=0, keepdims=False)
+        for piece in range(4)
+    ]
+    return jnp.concatenate(pieces, axis=0)
+
+
+def to_owners(grads):
+    row_y, row_x, core, line = place()
+    here = 2 * (line % 2) + core
+    pieces = to_half(grads).reshape(4, -1, grads.shape[1])
+    arrived = []
+    for turn in range(4):
+        piece = lax.dynamic_index_in_dim(pieces, (here - turn) % 4, axis=0, keepdims=False)
+        back = [(host, owner) for owner, host in column_pairs(turn)]
+        arrived.append(lax.ppermute(piece, COLUMN, back))
+    stacked = jnp.stack(arrived, axis=0)
+    parts = [
+        lax.dynamic_index_in_dim(stacked, (part - line) % 4, axis=0, keepdims=False)
+        for part in range(4)
+    ]
+    return jnp.concatenate(parts, axis=1).astype(jnp.float32)
+
+
+BIAS_PAIRS = [(i, (i % 2) * 4 + i // 2) for i in range(8)]
+
+
+def body_column(
+    tokens,
+    cotangent,
+    expert_ids,
+    slot_pos,
+    qkv_w,
+    qkv_m,
+    qkv_v,
+    out_w,
+    out_m,
+    out_v,
+    vectors,
+    vec_m,
+    vec_v,
+    w_in,
+    w_in_m,
+    w_in_v,
+    w_out,
+    w_out_m,
+    w_out_v,
+    b_in,
+    b_in_m,
+    b_in_v,
+):
+    f32 = jnp.float32
+    shard = jnp.concatenate(
+        [
+            to_half(qkv_w),
+            to_half(out_w),
+            jnp.pad(to_half(vectors.T), ((0, 0), (0, WIDE - 4 * D - vectors.shape[0]))),
+        ],
+        axis=1,
+    )
+    blocks = gather_line(shard)
+    blocks, w_in_now, w_out_now, b_in_now = lax.optimization_barrier(
+        (blocks, w_in, w_out, b_in)
+    )
+    gathered = gather_plane(blocks)
+    win_parts = to_hosts(w_in_now)
+    wout_parts = to_hosts(w_out_now.T)
+    bias_in = lax.ppermute(to_half(b_in_now), COLUMN, BIAS_PAIRS).astype(f32)
+
+    order = row_order()
+    qkv_half = gathered[:, : 3 * D]
+    out_half = gathered[:, 3 * D : 4 * D]
+    vec_real = exact_dot(gathered[:, 4 * D :], order, ((0,), (0,)))[:39]
+    router_half = to_half(vec_real[7 : 7 + EXPERTS])
+    out_bias = to_half(vec_real[7 + EXPERTS :])
+
+    normed_one, inv_one = normalize(tokens)
+    attn_in = to_half(normed_one * vec_real[0] + vec_real[1])
+    attn_rel = to_half(exact_dot(attn_in, order, ((1,), (1,))))
+    projected = jnp.dot(attn_rel, qkv_half, preferred_element_type=f32)
+    queries = to_half((projected[:, :D] + vec_real[4]) * HEAD ** (-0.5))
+    keys_b = to_half(projected[:, D : 2 * D])
+    values_b = to_half(projected[:, 2 * D :] + vec_real[5])
+    scores = jnp.einsum(
+        "ishd,ithd->ihst", heads_split(queries), heads_split(keys_b), preferred_element_type=f32
+    )
+    log_total = jnp.log(jnp.sum(jnp.exp(scores), axis=-1))
+    prob_half = to_half(jnp.exp(scores - log_total[..., None]))
+    head_mix = to_half(
+        jnp.einsum(
+            "ihst,ithd->ishd", prob_half, heads_split(values_b), preferred_element_type=f32
+        ).reshape(-1, D)
+    )
+    mix_rel = to_half(exact_dot(head_mix, order, ((1,), (1,))))
+    hidden_res = tokens + jnp.dot(mix_rel, out_half, preferred_element_type=f32) + vec_real[6]
+    normed_two, inv_two = normalize(hidden_res)
+    moe_in = to_half(normed_two * vec_real[2] + vec_real[3])
+    exp_logit = jnp.exp(exact_dot(moe_in, router_half, ((1,), (1,))))
+    route_prob = exp_logit / jnp.sum(exp_logit, axis=-1, keepdims=True)
+
+    kept_mask = slot_pos >= 0
+    onehot = expert_table(expert_ids)
+    slot_hits = to_half(slot_table(expert_ids, slot_pos)[0])
+    hits_both = slot_hits[:, 0] + slot_hits[:, 1]
+    gate_vals = jnp.where(kept_mask, jnp.sum(onehot * route_prob[:, None, :], axis=-1), 0.0)
+    packed = to_half(exact_dot(hits_both, moe_in, ((0,), (0,))))
+    weighted = to_half(gate_vals[..., None] * cotangent[:, None, :])
+    grad_packed = to_half(
+        exact_dot(slot_hits[:, 0], weighted[:, 0], ((0,), (0,)))
+        + exact_dot(slot_hits[:, 1], weighted[:, 1], ((0,), (0,)))
+    )
+    bias_grad = jnp.einsum(
+        "te,td->ed", jnp.sum(onehot * gate_vals[..., None], axis=1), cotangent, precision=EXACT
+    )
+
+    def both(first, second):
+        return jnp.concatenate(
+            [first.reshape(EXPERTS, CAP, D), second.reshape(EXPERTS, CAP, D)], axis=1
+        )
+
+    def swap_chips(rows):
+        return lax.all_to_all(rows, CHIPS, split_axis=0, concat_axis=0, tiled=True)
+
+    routed_own = swap_chips(both(packed, grad_packed))
+    routed = jnp.concatenate([routed_own, lax.ppermute(routed_own, "core", SWAP)], axis=0)
+    rows_in = routed[:, :CAP].reshape(-1, D)
+    grads_in = routed[:, CAP:].reshape(-1, D)
+
+    weight_in = settle(win_parts)
+    weight_out = settle(wout_parts)
+    pre_act = jnp.dot(rows_in, weight_in, preferred_element_type=f32) + bias_in[None, :]
+    activated, gelu_back = jax.vjp(jax.nn.gelu, pre_act)
+    act_half = to_half(activated)
+    expert_res = exact_dot(act_half, weight_out, ((1,), (1,)))
+    grad_act = exact_dot(grads_in, weight_out, ((1,), (0,)))
+    grad_wout = exact_dot(grads_in, act_half, ((0,), (0,)))
+    grad_pre = gelu_back(grad_act)[0]
+    grad_bias_in = jnp.sum(grad_pre, axis=0)
+    pre_half = to_half(grad_pre)
+    grad_win = exact_dot(rows_in, pre_half, ((0,), (0,)))
+    grad_slots = exact_dot(pre_half, weight_in, ((1,), (1,)))
+
+    def halves_sum(rows):
+        count = rows.shape[0] // 2
+        return to_half(rows[:count] + lax.ppermute(to_half(rows[count:]), "core", SWAP))
+
+    returned = swap_chips(both(halves_sum(expert_res), halves_sum(grad_slots)))
+    combined = returned[:, :CAP].reshape(-1, D)
+    slot_grads = returned[:, CAP:].reshape(-1, D)
+    w_out_grad = to_owners(grad_wout).T
+    w_in_grad = to_owners(grad_win)
+    b_in_grad = lax.ppermute(grad_bias_in, COLUMN, [(host, owner) for owner, host in BIAS_PAIRS])
+
+    onehot_half = to_half(onehot)
+    chosen = jnp.stack(
+        [
+            exact_dot(slot_hits[:, k], combined, ((1,), (0,)))
+            + exact_dot(onehot_half[:, k], out_bias, ((1,), (0,)))
+            for k in range(2)
+        ],
+        axis=1,
+    )
+    block_out = hidden_res + jnp.sum(gate_vals[..., None] * chosen, axis=1)
+    grad_gate = jnp.where(kept_mask, jnp.sum(cotangent[:, None, :] * chosen, axis=-1), 0.0)
+    grad_moe = exact_dot(hits_both, slot_grads, ((1,), (0,)))
+
+    grad_prob = jnp.sum(grad_gate[..., None] * onehot, axis=1)
+    grad_logit = route_prob * (grad_prob - jnp.sum(route_prob * grad_prob, axis=-1, keepdims=True))
+    logit_half = to_half(grad_logit)
+    router_grad = exact_dot(logit_half, moe_in, ((0,), (0,)))
+    grad_moe = grad_moe + jnp.dot(logit_half, router_half, preferred_element_type=f32)
+    gain_two = jnp.sum(grad_moe * normed_two, axis=0)
+    shift_two = jnp.sum(grad_moe, axis=0)
+    grad_res = cotangent + normalize_back(grad_moe * vec_real[2], normed_two, inv_two)
+    res_half = to_half(grad_res)
+    bias_out = jnp.sum(grad_res, axis=0)
+    out_part = exact_dot(mix_rel, res_half, ((0,), (0,)))
+    mix_back = to_half(exact_dot(res_half, out_half, ((1,), (1,))))
+    grad_mix = to_half(jnp.dot(mix_back, order, preferred_element_type=f32))
+    prob_full = jnp.exp(scores - log_total[..., None])
+    prob_half = to_half(prob_full)
+    grad_probs = jnp.einsum(
+        "ishd,ithd->ihst", heads_split(grad_mix), heads_split(values_b), preferred_element_type=f32
+    )
+    grad_values = jnp.einsum(
+        "ihst,ishd->ithd", prob_half, heads_split(grad_mix), preferred_element_type=f32
+    )
+    grad_scores = prob_full * (grad_probs - jnp.sum(prob_full * grad_probs, axis=-1, keepdims=True))
+    score_half = to_half(grad_scores)
+    grad_queries = jnp.einsum(
+        "ihst,ithd->ishd", score_half, heads_split(keys_b), preferred_element_type=f32
+    ) * HEAD ** (-0.5)
+    grad_keys = jnp.einsum(
+        "ihst,ishd->ithd", score_half, heads_split(queries), preferred_element_type=f32
+    )
+    grad_queries = grad_queries.reshape(-1, D)
+    grad_values = grad_values.reshape(-1, D)
+    proj_half = to_half(
+        jnp.concatenate([grad_queries, grad_keys.reshape(-1, D), grad_values], axis=1)
+    )
+    qkv_part = exact_dot(attn_rel, proj_half, ((0,), (0,)))
+    attn_back = exact_dot(proj_half, qkv_half, ((1,), (1,)))
+    grad_attn = jnp.dot(attn_back, order.astype(f32), precision=EXACT)
+    gain_one = jnp.sum(grad_attn * normed_one, axis=0)
+    shift_one = jnp.sum(grad_attn, axis=0)
+    input_grad = grad_res + normalize_back(grad_attn * vec_real[0], normed_one, inv_one)
+    small_part = jnp.stack(
+        [
+            gain_one,
+            shift_one,
+            gain_two,
+            shift_two,
+            jnp.sum(grad_queries, axis=0),
+            jnp.sum(grad_values, axis=0),
+            bias_out,
+        ]
+    )
+    vec_part = to_half(jnp.concatenate([small_part, router_grad, bias_grad], axis=0))
+    vec_rel = to_half(exact_dot(order, vec_part, ((1,), (1,))))
+    summed = scatter_sum(
+        jnp.concatenate(
+            [
+                to_half(qkv_part),
+                to_half(out_part),
+                jnp.pad(vec_rel, ((0, 0), (0, WIDE - 4 * D - vec_rel.shape[1]))),
+            ],
+            axis=1,
+        )
+    )
+    qkv_grad = summed[:, : 3 * D]
+    out_grad = summed[:, 3 * D : 4 * D]
+    vec_grad = summed[:, 4 * D : 4 * D + vectors.shape[0]].T
+    branch_bias_grad = jnp.concatenate([vec_grad[6:7], vec_grad[7 + EXPERTS :]], axis=0)
+    qkv_new, qkv_m_new, qkv_v_new = adamw_step(qkv_w, qkv_grad, qkv_m, qkv_v)
+    out_new, out_m_new, out_v_new = adamw_step(out_w, out_grad, out_m, out_v)
+    vec_new, vec_m_new, vec_v_new = adamw_step(vectors, vec_grad, vec_m, vec_v)
+    w_in_new, w_in_m_new, w_in_v_new = adamw_step(w_in, w_in_grad, w_in_m, w_in_v)
+    w_out_new, w_out_m_new, w_out_v_new = adamw_step(w_out, w_out_grad, w_out_m, w_out_v)
+    b_in_new, b_in_m_new, b_in_v_new = adamw_step(b_in, b_in_grad, b_in_m, b_in_v)
+    return (
+        block_out,
+        input_grad,
+        qkv_grad,
+        qkv_new,
+        qkv_m_new,
+        qkv_v_new,
+        out_grad,
+        out_new,
+        out_m_new,
+        out_v_new,
+        vec_grad,
+        vec_new,
+        vec_m_new,
+        vec_v_new,
+        w_in_grad,
+        w_in_new,
+        w_in_m_new,
+        w_in_v_new,
+        w_out_grad,
+        w_out_new,
+        w_out_m_new,
+        w_out_v_new,
+        b_in_grad,
+        b_in_new,
+        b_in_m_new,
+        b_in_v_new,
+        branch_bias_grad,
+    )
+
+
 def solution(mesh):
+    if mesh.shape["dp"] == 8 and mesh.shape["group"] == 4:
+        inner = Mesh(mesh.devices.reshape(2, 2, 2, 4), AXES)
+        body, dp, group, both = body_column, ("y", "x", "core"), "group", AXES
+    else:
+        inner, body, dp, group, both = mesh, body_any, "dp", "group", ("dp", "group")
     return jax.shard_map(
         body,
-        mesh=mesh,
+        mesh=inner,
         in_specs=(
-            P(("dp", "group"), None),
-            P(("dp", "group"), None),
-            P(("dp", "group"), None),
-            P(("dp", "group"), None),
-            P(("dp", "group"), None),
-            P(("dp", "group"), None),
-            P(("dp", "group"), None),
-            P(("dp", "group"), None),
-            P(("dp", "group"), None),
-            P(("dp", "group"), None),
-            P(None, ("dp", "group")),
-            P(None, ("dp", "group")),
-            P(None, ("dp", "group")),
-            P("group", "dp"),
-            P("group", "dp"),
-            P("group", "dp"),
-            P("dp", "group"),
-            P("dp", "group"),
-            P("dp", "group"),
-            P(("dp", "group")),
-            P(("dp", "group")),
-            P(("dp", "group")),
+            P(both, None),
+            P(both, None),
+            P(both, None),
+            P(both, None),
+            P(both, None),
+            P(both, None),
+            P(both, None),
+            P(both, None),
+            P(both, None),
+            P(both, None),
+            P(None, both),
+            P(None, both),
+            P(None, both),
+            P(group, dp),
+            P(group, dp),
+            P(group, dp),
+            P(dp, group),
+            P(dp, group),
+            P(dp, group),
+            P(both),
+            P(both),
+            P(both),
         ),
         out_specs=(
-            P(("dp", "group"), None),
-            P(("dp", "group"), None),
-            P(("dp", "group"), None),
-            P(("dp", "group"), None),
-            P(("dp", "group"), None),
-            P(("dp", "group"), None),
-            P(("dp", "group"), None),
-            P(("dp", "group"), None),
-            P(("dp", "group"), None),
-            P(("dp", "group"), None),
-            P(None, ("dp", "group")),
-            P(None, ("dp", "group")),
-            P(None, ("dp", "group")),
-            P(None, ("dp", "group")),
-            P("group", "dp"),
-            P("group", "dp"),
-            P("group", "dp"),
-            P("group", "dp"),
-            P("dp", "group"),
-            P("dp", "group"),
-            P("dp", "group"),
-            P("dp", "group"),
-            P(("dp", "group")),
-            P(("dp", "group")),
-            P(("dp", "group")),
-            P(("dp", "group")),
-            P(None, ("dp", "group")),
+            P(both, None),
+            P(both, None),
+            P(both, None),
+            P(both, None),
+            P(both, None),
+            P(both, None),
+            P(both, None),
+            P(both, None),
+            P(both, None),
+            P(both, None),
+            P(None, both),
+            P(None, both),
+            P(None, both),
+            P(None, both),
+            P(group, dp),
+            P(group, dp),
+            P(group, dp),
+            P(group, dp),
+            P(dp, group),
+            P(dp, group),
+            P(dp, group),
+            P(dp, group),
+            P(both),
+            P(both),
+            P(both),
+            P(both),
+            P(None, both),
         ),
         check_vma=False,
     )

time: 1340 us -> 494 us (0.37)
  waiting for transfers between devices: 934 us -> 91 us
  starting transfers between devices: 17.4 us -> 205 us
  blocking collectives: 103 us -> 0 us
  local copies, waits for them, and re-layouts: 123 us -> 62.3 us
    reduce_scatter x4 -> x0, waiting for transfers between devices: 546 us -> none  [the longest x1 161 us: body(): lax.psum_scatter(grad_win.transpose(1, 0, 2).reshape(D, hid_cols).astype(...]
    all_gather x4 -> x0, waiting for transfers between devices: 311 us -> none  [the longest x1 166 us: body(): lax.all_gather(to_half(w_out), 'group', axis=1, tiled=True)]
    ppermute x0 -> x39, starting transfers between devices: none -> 181 us  [the longest x8 83.6 us: to_owners(): arrived.append(lax.ppermute(piece, COLUMN, back))]
    ppermute x0 -> x39, waiting for transfers between devices: none -> 91 us  [the longest x8 36.8 us: to_hosts(): arrived.append(lax.ppermute(to_half(part), COLUMN, column_pairs(turn)))]
    all_gather x2 -> x0, blocking collectives: 87.1 us -> none  [the longest x1 71.7 us: body(): lax.all_gather(vec_shard, ('dp', 'group'), axis=1, tiled=True)]
    unnamed x10 -> x0, waiting for transfers between devices: 58.4 us -> none
    convert_element_type x6 -> x0, local copies, waits for them, and re-layouts: 28.4 us -> none  [the longest x1 12.7 us: body(): grad_win.transpose(1, 0, 2).reshape(D, hid_cols).astype(jnp.bfloat16)]
    all_gather x2 -> x0, local copies, waits for them, and re-layouts: 25.5 us -> none  [the longest x1 12.8 us: body(): lax.all_gather(to_half(w_out), 'group', axis=1, tiled=True)]
  transfers between devices with their start and end apart: 13 -> 41, of which waited for: 11 -> 14; matrix products, arithmetic and copies ran while one was open for 8% -> 29% of each run, Pallas kernels for 0% -> 0%
where the time goes in v1:
time: 494 us; the launch traced here: 485 us
  starting transfers between devices  205 us (41%)
  waiting for transfers between devices  91 us (18%)
  matrix products  69.6 us (14%)
  local copies, waits for them, and re-layouts  62.3 us (13%)
  other arithmetic  54.2 us (11%)
    ppermute x8, starting transfers between devices, to_owners(): arrived.append(lax.ppermute(piece, COLUMN, back))  83.6 us
    ppermute x8, starting transfers between devices, to_hosts(): arrived.append(lax.ppermute(to_half(part), COLUMN, column_pairs(turn)))  64.8 us
    dot_general x22, matrix products, exact_dot(): lax.dot_general(left, right, (dims, ((), ())), preferred_element_type=jnp...  39.1 us
    ppermute x8, waiting for transfers between devices, to_hosts(): arrived.append(lax.ppermute(to_half(part), COLUMN, column_pairs(turn)))  36.8 us
    sub x6, other arithmetic, adamw_step(): weight - LEARN_RATE * (step_dir + WEIGHT_DECAY * weight)  23.8 us
    all_to_all x2, starting transfers between devices, swap_chips(): return lax.all_to_all(rows, CHIPS, split_axis=0, concat_axis=0, tiled=True)  23.7 us
    ppermute x6, waiting for transfers between devices, join_swap(): return jnp.concatenate([rows, lax.ppermute(rows, axis_name, SWAP)], axis=0)  21.7 us
    ppermute x6, waiting for transfers between devices, fold_swap(): arrived = lax.ppermute(rows[half:], axis_name, SWAP)  17.8 us
  transfers between devices with their start and end apart: 41, of which 14 were waited for; matrix products, arithmetic and copies ran while one was open for 29% of the time, Pallas kernels for 0%

profile of v1, /device:TPU:0, one launch (start us, length us, event | category | flops | bytes accessed | tf_op | source)
XLA Modules:
  0.0 484.8 jit_solution(17415616696698643741)
XLA Ops:
  3.2 3.1 collective-permute-start
  6.3 2.6 collective-permute-start.1
  13.5 5.5 %collective-permute-done.1 = bf16[24,3200]{1,0:T(8,128)(2,1)S(1)} collective-permute-done((bf16[24,3200]{1,0:T(8,128)(2,1)S(1)}, bf16[24,3200]{1,0:T(8,128)(2,1)S(1)}, u32[]{:S(2)}, u32[]{:S(2)}) %collective-permute-start.1) | collective-permute-done | bytes 153632 | tf_op jit(solution)/shard_map/ppermute | solution.py:436
  20.6 1.6 collective-permute-start.6
  22.2 6.0 %collective-permute-done.3 = bf16[48,3200]{1,0:T(8,128)(2,1)S(1)} collective-permute-done((bf16[48,3200]{1,0:T(8,128)(2,1)S(1)}, bf16[48,3200]{1,0:T(8,128)(2,1)S(1)}, u32[]{:S(2)}, u32[]{:S(2)}) %collective-permute-start.3) | collective-permute-done | bytes 307232 | tf_op jit(solution)/shard_map/ppermute | solution.py:432
  28.3 1.6 collective-permute-start.4
  31.5 11.7 %collective-permute-done.4 = bf16[96,3200]{1,0:T(8,128)(2,1)S(1)} collective-permute-done((bf16[96,3200]{1,0:T(8,128)(2,1)S(1)}, bf16[96,3200]{1,0:T(8,128)(2,1)S(1)}, u32[]{:S(2)}, u32[]{:S(2)}) %collective-permute-start.4) | collective-permute-done | bytes 614432 | tf_op jit(solution)/shard_map/ppermute | solution.py:432
  51.4 2.0 fusion.157
  53.4 3.3 convolution_convert_fusion.6
  57.5 1.9 fusion.151
  64.8 2.5 pad_maximum_fusion.6
  67.4 7.6 %all-to-all-start = ((bf16[16,50,768]{2,1,0:T(8,128)(2,1)}), bf16[16,50,768]{2,1,0:T(8,128)(2,1)}, u32[]{:S(2)}, u32[]{:S(2)}) async-start(bf16[16,50,768]{2,1,0:T(8,128)(2,1)} %pad_maximum_fusion.6), calls=%async_computation | async-start | bytes 2752512 | tf_op jit(solution)/shard_map/all_to_all | solution.py:624
  75.0 3.5 reshape.366
  78.5 4.7 reshape.367
  83.2 15.4 %dynamic-slice_convert_fusion.3 = (bf16[192,1,1536]{2,1,0:T(2,128)(2,1)S(1)}, bf16[192,1,1536]{2,1,0:T(2,128)(2,1)S(1)}, bf16[192,1,1536]{2,1,0:T(2,128)(2,1)S(1...) fusion(bf16[192,4,1536]{2,1,0:T(4,128)(2,1)} %reshape.367, ...), kind=kLoop, calls=%fused_computation.95 | loop fusion | bytes 9437200 | tf_op jit(solution)/shard_map/convert_element_type | solution.py:27
  99.5 6.2 %collective-permute-start.11 = (bf16[192,1536]{1,0:T(8,128)(2,1)S(1)}, bf16[192,1536]{1,0:T(8,128)(2,1)S(1)}, u32[]{:S(2)}, u32[]{:S(2)}) collective-permute-start(bf16[192,1536]{1,0:T(8,128)(2,1)S(1)} %bitcast.221), channel_id=1, source_target_pairs={{0,4},{1,1},{2,5},{3,0},{4,6},{5,3},{6,7},{7,2},{8,12},{9,9},{10,1... | collective-permute-start | bytes 1769480 | tf_op jit(solution)/shard_map/ppermute | solution.py:495
  106.7 3.8 collective-permute-start.13
  114.8 6.0 %collective-permute-start.15 = (bf16[192,1536]{1,0:T(8,128)(2,1)}, bf16[192,1536]{1,0:T(8,128)(2,1)}, u32[]{:S(2)}, u32[]{:S(2)}) collective-permute-start(bf16[192,1536]{1,0:T(8,128)(2,1)} %bitcast.190), channel_id=1, source_target_pairs={{0,0},{1,4},{2,1},{3,5},{4,2},{5,6},{6,3},{7,7},{8,8},{9,12},{10,9... | collective-permute-start | bytes 1769480 | tf_op jit(solution)/shard_map/ppermute | solution.py:495
  120.7 41.3 %collective-permute-start.16 = (bf16[192,1536]{1,0:T(8,128)(2,1)}, bf16[192,1536]{1,0:T(8,128)(2,1)}, u32[]{:S(2)}, u32[]{:S(2)}) collective-permute-start(bf16[192,1536]{1,0:T(8,128)(2,1)} %bitcast.189), channel_id=1, source_target_pairs={{0,4},{1,1},{2,5},{3,0},{4,6},{5,3},{6,7},{7,2},{8,12},{9,9},{10,1... | collective-permute-start | bytes 1769480 | tf_op jit(solution)/shard_map/ppermute | solution.py:495
  162.1 4.9 %collective-permute-start.17 = (bf16[192,1536]{1,0:T(8,128)(2,1)}, bf16[192,1536]{1,0:T(8,128)(2,1)}, u32[]{:S(2)}, u32[]{:S(2)}) collective-permute-start(bf16[192,1536]{1,0:T(8,128)(2,1)} %bitcast.188), channel_id=1, source_target_pairs={{0,1},{1,5},{2,0},{3,4},{4,3},{5,7},{6,2},{7,6},{8,9},{9,13},{10,8... | collective-permute-start | bytes 1769480 | tf_op jit(solution)/shard_map/ppermute | solution.py:495
  167.0 1.9 collective-permute-start.18
  171.0 14.2 %collective-permute-done.16 = bf16[192,1536]{1,0:T(8,128)(2,1)} collective-permute-done((bf16[192,1536]{1,0:T(8,128)(2,1)}, bf16[192,1536]{1,0:T(8,128)(2,1)}, u32[]{:S(2)}, u32[]{:S(2)}) %collective-permute-start.16) | collective-permute-done | bytes 589856 | tf_op jit(solution)/shard_map/ppermute | solution.py:495
  185.2 22.5 %collective-permute-done.17 = bf16[192,1536]{1,0:T(8,128)(2,1)} collective-permute-done((bf16[192,1536]{1,0:T(8,128)(2,1)}, bf16[192,1536]{1,0:T(8,128)(2,1)}, u32[]{:S(2)}, u32[]{:S(2)}) %collective-permute-start.17) | collective-permute-done | bytes 589856 | tf_op jit(solution)/shard_map/ppermute | solution.py:495
  207.7 1.9 pad_maximum_fusion.2
  214.2 1.9 fusion.146
  216.1 2.4 reshape.365
  218.5 4.0 fusion.56
  222.6 3.1 fusion.55
  228.1 6.1 %collective-permute-start.19 = (bf16[400,768]{1,0:T(8,128)(2,1)}, bf16[400,768]{1,0:T(8,128)(2,1)S(1)}, u32[]{:S(2)}, u32[]{:S(2)}) collective-permute-start(bf16[400,768]{1,0:T(8,128)(2,1)} %slice.369), channel_id=1, source_target_pairs={{0,4},{4,0},{1,5},{5,1},{2,6},{6,2},{3,7},{7,3},{8,12},{12,8},{9,1... | collective-permute-start | bytes 1843208 | tf_op jit(solution)/shard_map/ppermute | solution.py:647
  235.5 7.3 %fusion.156 = (f32[1536]{0:T(1024)S(1)}, bf16[800,1536]{1,0:T(8,128)(2,1)S(1)}) fusion(f32[800,1536]{1,0:T(8,128)} %copy-done.75, f32[1536]{0:T(1024)S(1)} %convert_element_type.283, bf16[800,768]{1,0:T(8,128)(2,1)} %reshape.369, bf16[192,1536]{1,0:T(8,128)(2,1)} %get-tuple-element.326, bf16[192,1536]{1,0:T(8,128)(2,1)} %get-tuple-element.327, ...), kind=kOutput, calls=%fused_computation.351 | convolution fusion | flops 1923906048 | bytes 10973184 | tf_op jit(solution)/shard_map/dot_general | solution.py:420
  242.9 2.1 fusion.33
  252.8 16.1 %all-to-all-start.1 = ((bf16[16,50,768]{2,1,0:T(8,128)(2,1)}), bf16[16,50,768]{2,1,0:T(8,128)(2,1)S(1)}, u32[]{:S(2)}, u32[]{:S(2)}) async-start(bf16[16,50,768]{2,1,0:T(8,128)(2,1)} %pad_maximum_fusion.7), calls=%async_computation.1 | async-start | bytes 2752512 | tf_op jit(solution)/shard_map/all_to_all | solution.py:624
  268.9 5.7 %convolution_convert_fusion.1 = bf16[768,1536]{1,0:T(8,128)(2,1)S(1)} fusion(bf16[800,768]{1,0:T(8,128)(2,1)} %reshape.369, f32[800,1536]{1,0:T(8,128)} %copy-done.75, f32[1536]{0:T(1024)S(1)} %convert_element_type.283), kind=kOutput, calls=%fused_computation.23 | convolution fusion | flops 1900904448 | bytes 8509440 | tf_op jit(solution)/shard_map/dot_general | solution.py:420
  275.7 7.0 %collective-permute-start.35 = (bf16[192,1536]{1,0:T(8,128)(2,1)S(1)}, bf16[192,1536]{1,0:T(8,128)(2,1)S(1)}, u32[]{:S(2)}, u32[]{:S(2)}) collective-permute-start(bf16[192,1536]{1,0:T(8,128)(2,1)S(1)} %get-tuple-element.316), channel_id=1, source_target_pairs={{4,0},{1,1},{5,2},{0,3},{6,4},{3,5},{7,6},{2,7},{12,8},{9,9},{13,1... | collective-permute-start | bytes 1769480 | tf_op jit(solution)/shard_map/ppermute | solution.py:518
  282.8 3.9 collective-permute-start.37
  286.7 2.9 convolution_convert_fusion.2
  291.8 6.0 %collective-permute-start.30 = (bf16[192,1536]{1,0:T(8,128)(2,1)}, bf16[192,1536]{1,0:T(8,128)(2,1)}, u32[]{:S(2)}, u32[]{:S(2)}) collective-permute-start(bf16[192,1536]{1,0:T(8,128)(2,1)} %get-tuple-element.321), channel_id=1, source_target_pairs={{0,0},{4,1},{1,2},{5,3},{2,4},{6,5},{3,6},{7,7},{8,8},{12,9},{9,10... | collective-permute-start | bytes 1769480 | tf_op jit(solution)/shard_map/ppermute | solution.py:518
  298.4 60.1 %collective-permute-start.31 = (bf16[192,1536]{1,0:T(8,128)(2,1)}, bf16[192,1536]{1,0:T(8,128)(2,1)}, u32[]{:S(2)}, u32[]{:S(2)}) collective-permute-start(bf16[192,1536]{1,0:T(8,128)(2,1)} %get-tuple-element.324), channel_id=1, source_target_pairs={{4,0},{1,1},{5,2},{0,3},{6,4},{3,5},{7,6},{2,7},{12,8},{9,9},{13,1... | collective-permute-start | bytes 1769480 | tf_op jit(solution)/shard_map/ppermute | solution.py:518
  359.7 4.5 collective-permute-start.33
  372.6 2.2 reshape.372
  376.1 1.9 multiply_reduce_fusion.3
  378.0 1.7 fusion.144
  379.7 2.4 fusion.37
  383.1 1.6 fusion.158
  384.7 2.7 multiply_reduce_fusion
  387.4 2.2 multiply_convert_fusion.1
  391.3 4.8 fusion.148
  397.5 4.0 convolution_convert_fusion
  401.5 3.5 fusion.11
  405.2 2.7 multiply_reduce_fusion.4
  409.9 3.2 fusion.8
  413.2 1.6 fusion.145
  415.6 10.4 %multiply_subtract_fusion = (f32[6144,192]{0,1:T(8,128)}, f32[6144,192]{0,1:T(8,128)}, f32[6144,192]{0,1:T(8,128)}, f32[6144,192]{0,1:T(8,128)}) fusion(f32[6144,192]{0,1:T(8,128)S(1)} %bitcast.197, f32[6144,192]{0,1:T(8,128)} %param.39, f32[6144,192]{0,1:T(8,128)} %param.40, bf16[192,1536]{1,0:T(8,128)(2,1)S(1)} %copy-done.12, ...), kind=kLoop, calls=%fused_computation.19 | loop fusion | flops 27131904 | bytes 35389440 | tf_op jit(solution)/shard_map/sub | solution.py:200
  426.1 1.9 pad_maximum_fusion.4
  428.2 2.4 add_convert_fusion.1
  430.6 1.7 collective-permute-start.22
  432.4 10.4 %multiply_subtract_fusion.1 = (f32[192,6144]{1,0:T(8,128)}, f32[192,6144]{1,0:T(8,128)}, f32[192,6144]{1,0:T(8,128)}, f32[192,6144]{1,0:T(8,128)}) fusion(f32[192,6144]{1,0:T(8,128)S(1)} %bitcast.199, f32[192,6144]{1,0:T(8,128)} %param.36, f32[192,6144]{1,0:T(8,128)} %param.37, bf16[192,1536]{1,0:T(8,128)(2,1)S(1)} %get-tuple-element.318, ...), kind=kLoop, calls=%fused_computation.21 | loop fusion | flops 27131904 | bytes 35389440 | tf_op jit(solution)/shard_map/sub | solution.py:200
  444.4 1.8 collective-permute-done.22
  446.4 1.7 collective-permute-start.23
  448.1 11.6 %collective-permute-done.26 = bf16[96,3200]{1,0:T(8,128)(2,1)S(1)} collective-permute-done((bf16[96,3200]{1,0:T(8,128)(2,1)S(1)}, bf16[96,3200]{1,0:T(8,128)(2,1)S(1)}, u32[]{:S(2)}, u32[]{:S(2)}) %collective-permute-start.26) | collective-permute-done | bytes 614432 | tf_op jit(solution)/shard_map/ppermute | solution.py:449
  460.3 4.4 collective-permute-done.23
  464.9 2.9 collective-permute-start.24
  468.6 2.3 collective-permute-start.29
  472.2 8.2 %collective-permute-done.28 = bf16[24,3200]{1,0:T(8,128)(2,1)S(1)} collective-permute-done((bf16[24,3200]{1,0:T(8,128)(2,1)S(1)}, bf16[24,3200]{1,0:T(8,128)(2,1)S(1)}, u32[]{:S(2)}, u32[]{:S(2)}) %collective-permute-start.28) | collective-permute-done | bytes 153632 | tf_op jit(solution)/shard_map/ppermute | solution.py:461
  (351 shorter events, 78.9 us)
Async XLA Ops:
  3.2 10.3 %collective-permute-start = (bf16[24,3200]{1,0:T(8,128)(2,1)S(1)}, bf16[24,3200]{1,0:T(8,128)(2,1)S(1)}, u32[]{:S(2)}, u32[]{:S(2)}) collective-permute-start(bf16[24,3200]{1,0:T(8,128)(2,1)S(1)} %fusion.85), channel_id=1, source_target_pairs={{0,1},{1,2},{2,3},{3,0},{4,5},{5,6},{6,7},{7,4},{8,9},{9,10},{10,1... | collective-permute-start | bytes 460808 | tf_op jit(solution)/shard_map/ppermute | solution.py:436
  6.3 12.7 %collective-permute-start.1 = (bf16[24,3200]{1,0:T(8,128)(2,1)S(1)}, bf16[24,3200]{1,0:T(8,128)(2,1)S(1)}, u32[]{:S(2)}, u32[]{:S(2)}) collective-permute-start(bf16[24,3200]{1,0:T(8,128)(2,1)S(1)} %fusion.85), channel_id=1, source_target_pairs={{0,2},{1,3},{2,0},{3,1},{4,6},{5,7},{6,4},{7,5},{8,10},{9,11},{10,... | collective-permute-start | bytes 460808 | tf_op jit(solution)/shard_map/ppermute | solution.py:436
  8.9 10.1 %collective-permute-start.2 = (bf16[24,3200]{1,0:T(8,128)(2,1)S(1)}, bf16[24,3200]{1,0:T(8,128)(2,1)S(1)}, u32[]{:S(2)}, u32[]{:S(2)}) collective-permute-start(bf16[24,3200]{1,0:T(8,128)(2,1)S(1)} %fusion.85), channel_id=1, source_target_pairs={{0,3},{1,0},{2,1},{3,2},{4,7},{5,4},{6,5},{7,6},{8,11},{9,8},{10,9... | collective-permute-start | bytes 460808 | tf_op jit(solution)/shard_map/ppermute | solution.py:436
  11.5 37.5 %copy-start.56 = (f32[197]{0:T(256)}, f32[197]{0:T(256)S(1)}, u32[]{:S(2)}) copy-start(f32[197]{0:T(256)S(1)} %broadcast_multiply_fusion.5) | copy-start | bytes 2368
  13.5 35.5 %copy-start.64 = (f32[197]{0:T(256)}, f32[197]{0:T(256)S(1)}, u32[]{:S(2)}) copy-start(f32[197]{0:T(256)S(1)} %add_rsqrt_fusion.1) | copy-start | bytes 2368
  13.5 366.2 %copy-start.68 = (s32[768]{0:T(1024)}, s32[768]{0:T(1024)S(1)}, u32[]{:S(2)}) copy-start(s32[768]{0:T(1024)S(1)} %fusion.117) | copy-start | bytes 9220
  19.0 9.2 %collective-permute-start.3 = (bf16[48,3200]{1,0:T(8,128)(2,1)S(1)}, bf16[48,3200]{1,0:T(8,128)(2,1)S(1)}, u32[]{:S(2)}, u32[]{:S(2)}) collective-permute-start(bf16[48,3200]{1,0:T(8,128)(2,1)S(1)} %pad_maximum_fusion.22), channel_id=1, source_target_pairs={{0,8},{8,0},{1,9},{9,1},{2,10},{10,2},{3,11},{11,3},{4,12},{12,4},... | collective-permute-start | bytes 921608 | tf_op jit(solution)/shard_map/ppermute | solution.py:432
  20.6 9.2 %collective-permute-start.6 = (bf16[48,3200]{1,0:T(8,128)(2,1)S(1)}, bf16[48,3200]{1,0:T(8,128)(2,1)S(1)}, u32[]{:S(2)}, u32[]{:S(2)}) collective-permute-start(bf16[48,3200]{1,0:T(8,128)(2,1)S(1)} %pad_maximum_fusion.23), channel_id=1, source_target_pairs={{0,16},{16,0},{1,17},{17,1},{2,18},{18,2},{3,19},{19,3},{4,20},{20... | collective-permute-start | bytes 921608 | tf_op jit(solution)/shard_map/ppermute | solution.py:432
  28.3 14.9 %collective-permute-start.4 = (bf16[96,3200]{1,0:T(8,128)(2,1)S(1)}, bf16[96,3200]{1,0:T(8,128)(2,1)S(1)}, u32[]{:S(2)}, u32[]{:S(2)}) collective-permute-start(bf16[96,3200]{1,0:T(8,128)(2,1)S(1)} %pad_maximum_fusion.12), channel_id=1, source_target_pairs={{0,16},{16,0},{1,17},{17,1},{2,18},{18,2},{3,19},{19,3},{4,20},{20... | collective-permute-start | bytes 1843208 | tf_op jit(solution)/shard_map/ppermute | solution.py:432
  29.9 14.6 %collective-permute-start.7 = (bf16[96,3200]{1,0:T(8,128)(2,1)S(1)}, bf16[96,3200]{1,0:T(8,128)(2,1)S(1)}, u32[]{:S(2)}, u32[]{:S(2)}) collective-permute-start(bf16[96,3200]{1,0:T(8,128)(2,1)S(1)} %pad_maximum_fusion.13), channel_id=1, source_target_pairs={{0,8},{8,0},{1,9},{9,1},{2,10},{10,2},{3,11},{11,3},{4,12},{12,4},... | collective-permute-start | bytes 1843208 | tf_op jit(solution)/shard_map/ppermute | solution.py:432
  43.2 3.0 collective-permute-start.5
  44.6 3.4 collective-permute-start.8
  48.8 11.0 %copy-start.50 = (bf16[128,768]{1,0:T(8,128)(2,1)}, bf16[128,768]{1,0:T(8,128)(2,1)S(1)}, u32[]{:S(2)}) copy-start(bf16[128,768]{1,0:T(8,128)(2,1)S(1)} %get-tuple-element.354) | copy-start | bytes 589828
  67.4 101.6 %all-to-all-start = ((bf16[16,50,768]{2,1,0:T(8,128)(2,1)}), bf16[16,50,768]{2,1,0:T(8,128)(2,1)}, u32[]{:S(2)}, u32[]{:S(2)}) async-start(bf16[16,50,768]{2,1,0:T(8,128)(2,1)} %pad_maximum_fusion.6), calls=%async_computation | async-start | bytes 2752512 | tf_op jit(solution)/shard_map/all_to_all | solution.py:624
  98.7 22.1 %collective-permute-start.10 = (bf16[192,1536]{1,0:T(8,128)(2,1)S(1)}, bf16[192,1536]{1,0:T(8,128)(2,1)S(1)}, u32[]{:S(2)}, u32[]{:S(2)}) collective-permute-start(bf16[192,1536]{1,0:T(8,128)(2,1)S(1)} %bitcast.222), channel_id=1, source_target_pairs={{0,0},{1,4},{2,1},{3,5},{4,2},{5,6},{6,3},{7,7},{8,8},{9,12},{10,9... | collective-permute-start | bytes 1769480 | tf_op jit(solution)/shard_map/ppermute | solution.py:495
  99.4 11.1 %copy-start.47 = (f32[1536]{0:T(1024)S(1)}, f32[1536]{0:T(1024)}, u32[]{:S(2)}) copy-start(f32[1536]{0:T(1024)} %param.41) | copy-start | bytes 18436
  99.5 62.6 %collective-permute-start.11 = (bf16[192,1536]{1,0:T(8,128)(2,1)S(1)}, bf16[192,1536]{1,0:T(8,128)(2,1)S(1)}, u32[]{:S(2)}, u32[]{:S(2)}) collective-permute-start(bf16[192,1536]{1,0:T(8,128)(2,1)S(1)} %bitcast.221), channel_id=1, source_target_pairs={{0,4},{1,1},{2,5},{3,0},{4,6},{5,3},{6,7},{7,2},{8,12},{9,9},{10,1... | collective-permute-start | bytes 1769480 | tf_op jit(solution)/shard_map/ppermute | solution.py:495
  105.7 61.2 %collective-permute-start.12 = (bf16[192,1536]{1,0:T(8,128)(2,1)S(1)}, bf16[192,1536]{1,0:T(8,128)(2,1)S(1)}, u32[]{:S(2)}, u32[]{:S(2)}) collective-permute-start(bf16[192,1536]{1,0:T(8,128)(2,1)S(1)} %bitcast.220), channel_id=1, source_target_pairs={{0,1},{1,5},{2,0},{3,4},{4,3},{5,7},{6,2},{7,6},{8,9},{9,13},{10,8... | collective-permute-start | bytes 1769480 | tf_op jit(solution)/shard_map/ppermute | solution.py:495
  106.7 63.9 %collective-permute-start.13 = (bf16[192,1536]{1,0:T(8,128)(2,1)}, bf16[192,1536]{1,0:T(8,128)(2,1)S(1)}, u32[]{:S(2)}, u32[]{:S(2)}) collective-permute-start(bf16[192,1536]{1,0:T(8,128)(2,1)} %bitcast.191), channel_id=1, source_target_pairs={{0,5},{1,0},{2,4},{3,1},{4,7},{5,2},{6,6},{7,3},{8,13},{9,8},{10,1... | collective-permute-start | bytes 1769480 | tf_op jit(solution)/shard_map/ppermute | solution.py:495
  110.5 4.2 collective-permute-start.14
  114.8 56.2 %collective-permute-start.15 = (bf16[192,1536]{1,0:T(8,128)(2,1)}, bf16[192,1536]{1,0:T(8,128)(2,1)}, u32[]{:S(2)}, u32[]{:S(2)}) collective-permute-start(bf16[192,1536]{1,0:T(8,128)(2,1)} %bitcast.190), channel_id=1, source_target_pairs={{0,0},{1,4},{2,1},{3,5},{4,2},{5,6},{6,3},{7,7},{8,8},{9,12},{10,9... | collective-permute-start | bytes 1769480 | tf_op jit(solution)/shard_map/ppermute | solution.py:495
  120.7 64.4 %collective-permute-start.16 = (bf16[192,1536]{1,0:T(8,128)(2,1)}, bf16[192,1536]{1,0:T(8,128)(2,1)}, u32[]{:S(2)}, u32[]{:S(2)}) collective-permute-start(bf16[192,1536]{1,0:T(8,128)(2,1)} %bitcast.189), channel_id=1, source_target_pairs={{0,4},{1,1},{2,5},{3,0},{4,6},{5,3},{6,7},{7,2},{8,12},{9,9},{10,1... | collective-permute-start | bytes 1769480 | tf_op jit(solution)/shard_map/ppermute | solution.py:495
  162.1 45.7 %collective-permute-start.17 = (bf16[192,1536]{1,0:T(8,128)(2,1)}, bf16[192,1536]{1,0:T(8,128)(2,1)}, u32[]{:S(2)}, u32[]{:S(2)}) collective-permute-start(bf16[192,1536]{1,0:T(8,128)(2,1)} %bitcast.188), channel_id=1, source_target_pairs={{0,1},{1,5},{2,0},{3,4},{4,3},{5,7},{6,2},{7,6},{8,9},{9,13},{10,8... | collective-permute-start | bytes 1769480 | tf_op jit(solution)/shard_map/ppermute | solution.py:495
  167.0 40.7 %collective-permute-start.18 = (bf16[192,1536]{1,0:T(8,128)(2,1)}, bf16[192,1536]{1,0:T(8,128)(2,1)}, u32[]{:S(2)}, u32[]{:S(2)}) collective-permute-start(bf16[192,1536]{1,0:T(8,128)(2,1)} %bitcast.187), channel_id=1, source_target_pairs={{0,5},{1,0},{2,4},{3,1},{4,7},{5,2},{6,6},{7,3},{8,13},{9,8},{10,1... | collective-permute-start | bytes 1769480 | tf_op jit(solution)/shard_map/ppermute | solution.py:495
  170.6 43.3 %collective-permute-start.9 = (bf16[16,50,768]{2,0,1:T(8,128)(2,1)S(1)}, bf16[16,50,768]{2,0,1:T(8,128)(2,1)S(1)}, u32[]{:S(2)}, u32[]{:S(2)}) collective-permute-start(bf16[16,50,768]{2,0,1:T(8,128)(2,1)S(1)} %copy.154), channel_id=1, source_target_pairs={{0,4},{4,0},{1,5},{5,1},{2,6},{6,2},{3,7},{7,3},{8,12},{12,8},{9,1... | collective-permute-start | bytes 3686408 | tf_op jit(solution)/shard_map/ppermute | solution.py:627
  228.1 19.3 %collective-permute-start.19 = (bf16[400,768]{1,0:T(8,128)(2,1)}, bf16[400,768]{1,0:T(8,128)(2,1)S(1)}, u32[]{:S(2)}, u32[]{:S(2)}) collective-permute-start(bf16[400,768]{1,0:T(8,128)(2,1)} %slice.369), channel_id=1, source_target_pairs={{0,4},{4,0},{1,5},{5,1},{2,6},{6,2},{3,7},{7,3},{8,12},{12,8},{9,1... | collective-permute-start | bytes 1843208 | tf_op jit(solution)/shard_map/ppermute | solution.py:647
  247.3 2.4 collective-permute-start.20
  252.8 113.3 %all-to-all-start.1 = ((bf16[16,50,768]{2,1,0:T(8,128)(2,1)}), bf16[16,50,768]{2,1,0:T(8,128)(2,1)S(1)}, u32[]{:S(2)}, u32[]{:S(2)}) async-start(bf16[16,50,768]{2,1,0:T(8,128)(2,1)} %pad_maximum_fusion.7), calls=%async_computation.1 | async-start | bytes 2752512 | tf_op jit(solution)/shard_map/all_to_all | solution.py:624
  274.6 12.1 %copy-start.21 = (bf16[800,768]{1,0:T(8,128)(2,1)S(1)}, bf16[800,768]{1,0:T(8,128)(2,1)}, u32[]{:S(2)}) copy-start(bf16[800,768]{1,0:T(8,128)(2,1)} %reshape.365) | copy-start | bytes 3686404
  274.6 12.1 %copy-start.77 = (bf16[800,1536]{1,0:T(8,128)(2,1)S(1)}, bf16[800,1536]{1,0:T(8,128)(2,1)}, u32[]{:S(2)}) copy-start(bf16[800,1536]{1,0:T(8,128)(2,1)} %copy-done.76) | copy-start | bytes 7372804
  274.8 23.6 %collective-permute-start.34 = (bf16[192,1536]{1,0:T(8,128)(2,1)S(1)}, bf16[192,1536]{1,0:T(8,128)(2,1)S(1)}, u32[]{:S(2)}, u32[]{:S(2)}) collective-permute-start(bf16[192,1536]{1,0:T(8,128)(2,1)S(1)} %get-tuple-element.313), channel_id=1, source_target_pairs={{0,0},{4,1},{1,2},{5,3},{2,4},{6,5},{3,6},{7,7},{8,8},{12,9},{9,10... | collective-permute-start | bytes 1769480 | tf_op jit(solution)/shard_map/ppermute | solution.py:518
  275.7 82.8 %collective-permute-start.35 = (bf16[192,1536]{1,0:T(8,128)(2,1)S(1)}, bf16[192,1536]{1,0:T(8,128)(2,1)S(1)}, u32[]{:S(2)}, u32[]{:S(2)}) collective-permute-start(bf16[192,1536]{1,0:T(8,128)(2,1)S(1)} %get-tuple-element.316), channel_id=1, source_target_pairs={{4,0},{1,1},{5,2},{0,3},{6,4},{3,5},{7,6},{2,7},{12,8},{9,9},{13,1... | collective-permute-start | bytes 1769480 | tf_op jit(solution)/shard_map/ppermute | solution.py:518
  282.7 77.0 %collective-permute-start.36 = (bf16[192,1536]{1,0:T(8,128)(2,1)S(1)}, bf16[192,1536]{1,0:T(8,128)(2,1)S(1)}, u32[]{:S(2)}, u32[]{:S(2)}) collective-permute-start(bf16[192,1536]{1,0:T(8,128)(2,1)S(1)} %get-tuple-element.315), channel_id=1, source_target_pairs={{1,0},{5,1},{0,2},{4,3},{3,4},{7,5},{2,6},{6,7},{9,8},{13,9},{8,10... | collective-permute-start | bytes 1769480 | tf_op jit(solution)/shard_map/ppermute | solution.py:518
  282.8 81.4 %collective-permute-start.37 = (bf16[192,1536]{1,0:T(8,128)(2,1)S(1)}, bf16[192,1536]{1,0:T(8,128)(2,1)S(1)}, u32[]{:S(2)}, u32[]{:S(2)}) collective-permute-start(bf16[192,1536]{1,0:T(8,128)(2,1)S(1)} %get-tuple-element.314), channel_id=1, source_target_pairs={{5,0},{0,1},{4,2},{1,3},{7,4},{2,5},{6,6},{3,7},{13,8},{8,9},{12,1... | collective-permute-start | bytes 1769480 | tf_op jit(solution)/shard_map/ppermute | solution.py:518
  289.7 8.1 %copy-start.61 = (f32[1536]{0:T(1024)S(1)}, f32[1536]{0:T(1024)}, u32[]{:S(2)}) copy-start(f32[1536]{0:T(1024)} %param.42) | copy-start | bytes 18436
  289.7 2.1 collective-permute-start.38
  291.8 74.3 %copy-start.48 = (f32[1536]{0:T(1024)}, f32[1536]{0:T(1024)S(1)}, u32[]{:S(2)}) copy-start(f32[1536]{0:T(1024)S(1)} %collective-permute-done.38) | copy-start | bytes 18436
  291.8 123.0 %collective-permute-start.30 = (bf16[192,1536]{1,0:T(8,128)(2,1)}, bf16[192,1536]{1,0:T(8,128)(2,1)}, u32[]{:S(2)}, u32[]{:S(2)}) collective-permute-start(bf16[192,1536]{1,0:T(8,128)(2,1)} %get-tuple-element.321), channel_id=1, source_target_pairs={{0,0},{4,1},{1,2},{5,3},{2,4},{6,5},{3,6},{7,7},{8,8},{12,9},{9,10... | collective-permute-start | bytes 1769480 | tf_op jit(solution)/shard_map/ppermute | solution.py:518
  298.4 127.6 %collective-permute-start.31 = (bf16[192,1536]{1,0:T(8,128)(2,1)}, bf16[192,1536]{1,0:T(8,128)(2,1)}, u32[]{:S(2)}, u32[]{:S(2)}) collective-permute-start(bf16[192,1536]{1,0:T(8,128)(2,1)} %get-tuple-element.324), channel_id=1, source_target_pairs={{4,0},{1,1},{5,2},{0,3},{6,4},{3,5},{7,6},{2,7},{12,8},{9,9},{13,1... | collective-permute-start | bytes 1769480 | tf_op jit(solution)/shard_map/ppermute | solution.py:518
  358.5 67.5 %collective-permute-start.32 = (bf16[192,1536]{1,0:T(8,128)(2,1)}, bf16[192,1536]{1,0:T(8,128)(2,1)}, u32[]{:S(2)}, u32[]{:S(2)}) collective-permute-start(bf16[192,1536]{1,0:T(8,128)(2,1)} %get-tuple-element.323), channel_id=1, source_target_pairs={{1,0},{5,1},{0,2},{4,3},{3,4},{7,5},{2,6},{6,7},{9,8},{13,9},{8,10... | collective-permute-start | bytes 1769480 | tf_op jit(solution)/shard_map/ppermute | solution.py:518
  359.7 66.3 %collective-permute-start.33 = (bf16[192,1536]{1,0:T(8,128)(2,1)}, bf16[192,1536]{1,0:T(8,128)(2,1)}, u32[]{:S(2)}, u32[]{:S(2)}) collective-permute-start(bf16[192,1536]{1,0:T(8,128)(2,1)} %get-tuple-element.322), channel_id=1, source_target_pairs={{5,0},{0,1},{4,2},{1,3},{7,4},{2,5},{6,6},{3,7},{13,8},{8,9},{12,1... | collective-permute-start | bytes 1769480 | tf_op jit(solution)/shard_map/ppermute | solution.py:518
  414.8 13.4 %collective-permute-start.21 = (bf16[192,3200]{1,0:T(8,128)(2,1)}, bf16[192,3200]{1,0:T(8,128)(2,1)}, u32[]{:S(2)}, u32[]{:S(2)}) collective-permute-start(bf16[192,3200]{1,0:T(8,128)(2,1)} %get-tuple-element.305), channel_id=1, source_target_pairs={{0,4},{4,0},{1,5},{5,1},{2,6},{6,2},{3,7},{7,3},{8,12},{12,8},{9,1... | collective-permute-start | bytes 3686408 | tf_op jit(solution)/shard_map/ppermute | solution.py:449
  414.8 13.4 %collective-permute-start.25 = (bf16[192,3200]{1,0:T(8,128)(2,1)}, bf16[192,3200]{1,0:T(8,128)(2,1)}, u32[]{:S(2)}, u32[]{:S(2)}) collective-permute-start(bf16[192,3200]{1,0:T(8,128)(2,1)} %get-tuple-element.306), channel_id=1, source_target_pairs={{0,4},{4,0},{1,5},{5,1},{2,6},{6,2},{3,7},{7,3},{8,12},{12,8},{9,1... | collective-permute-start | bytes 3686408 | tf_op jit(solution)/shard_map/ppermute | solution.py:449
  430.6 15.6 %collective-permute-start.22 = (bf16[96,3200]{1,0:T(8,128)(2,1)S(1)}, bf16[96,3200]{1,0:T(8,128)(2,1)S(1)}, u32[]{:S(2)}, u32[]{:S(2)}) collective-permute-start(bf16[96,3200]{1,0:T(8,128)(2,1)S(1)} %slice.259), channel_id=1, source_target_pairs={{0,16},{16,0},{1,17},{17,1},{2,18},{18,2},{3,19},{19,3},{4,20},{20... | collective-permute-start | bytes 1843208 | tf_op jit(solution)/shard_map/ppermute | solution.py:449
  432.4 10.4 %copy-start.71 = (f32[197]{0:T(256)S(1)}, f32[197]{0:T(256)}, u32[]{:S(2)}) copy-start(f32[197]{0:T(256)} %get-tuple-element.260) | copy-start | bytes 2368
  432.4 10.5 %copy-start.70 = (f32[197]{0:T(256)S(1)}, f32[197]{0:T(256)}, u32[]{:S(2)}) copy-start(f32[197]{0:T(256)} %get-tuple-element.263) | copy-start | bytes 2368
  442.9 16.9 %collective-permute-start.26 = (bf16[96,3200]{1,0:T(8,128)(2,1)S(1)}, bf16[96,3200]{1,0:T(8,128)(2,1)S(1)}, u32[]{:S(2)}, u32[]{:S(2)}) collective-permute-start(bf16[96,3200]{1,0:T(8,128)(2,1)S(1)} %slice.267), channel_id=1, source_target_pairs={{0,8},{8,0},{1,9},{9,1},{2,10},{10,2},{3,11},{11,3},{4,12},{12,4},... | collective-permute-start | bytes 1843208 | tf_op jit(solution)/shard_map/ppermute | solution.py:449
  446.4 24.5 %copy-start.25 = (f32[197,768]{1,0:T(8,128)S(1)}, f32[197,768]{1,0:T(8,128)}, u32[]{:S(2)}) copy-start(f32[197,768]{1,0:T(8,128)} %get-tuple-element.363) | copy-start | bytes 1815556
  446.4 24.5 %copy-start.66 = (f32[197]{0:T(256)S(1)}, f32[197]{0:T(256)}, u32[]{:S(2)}) copy-start(f32[197]{0:T(256)} %copy-done.64) | copy-start | bytes 2368
  446.4 18.4 %collective-permute-start.23 = (bf16[48,3200]{1,0:T(8,128)(2,1)S(1)}, bf16[48,3200]{1,0:T(8,128)(2,1)S(1)}, u32[]{:S(2)}, u32[]{:S(2)}) collective-permute-start(bf16[48,3200]{1,0:T(8,128)(2,1)S(1)} %slice.261), channel_id=1, source_target_pairs={{0,8},{8,0},{1,9},{9,1},{2,10},{10,2},{3,11},{11,3},{4,12},{12,4},... | collective-permute-start | bytes 921608 | tf_op jit(solution)/shard_map/ppermute | solution.py:449
  459.9 7.9 %collective-permute-start.27 = (bf16[48,3200]{1,0:T(8,128)(2,1)S(1)}, bf16[48,3200]{1,0:T(8,128)(2,1)S(1)}, u32[]{:S(2)}, u32[]{:S(2)}) collective-permute-start(bf16[48,3200]{1,0:T(8,128)(2,1)S(1)} %slice.269), channel_id=1, source_target_pairs={{0,16},{16,0},{1,17},{17,1},{2,18},{18,2},{3,19},{19,3},{4,20},{20... | collective-permute-start | bytes 921608 | tf_op jit(solution)/shard_map/ppermute | solution.py:449
  464.8 15.7 %copy-start.45 = (f32[39,24]{0,1:T(8,128)S(1)}, f32[39,24]{0,1:T(8,128)}, u32[]{:S(2)}) copy-start(f32[39,24]{0,1:T(8,128)} %param.32) | copy-start | bytes 11236
  464.9 15.7 %copy-start.54 = (f32[39,24]{0,1:T(8,128)S(1)}, f32[39,24]{0,1:T(8,128)}, u32[]{:S(2)}) copy-start(f32[39,24]{0,1:T(8,128)} %param.33) | copy-start | bytes 11236
  464.9 15.7 %copy-start.55 = (f32[39,24]{0,1:T(8,128)S(1)}, f32[39,24]{0,1:T(8,128)}, u32[]{:S(2)}) copy-start(f32[39,24]{0,1:T(8,128)} %param.34) | copy-start | bytes 11236
  464.9 17.2 %copy-start.24 = (f32[24,2304]{1,0:T(8,128)S(1)}, f32[24,2304]{1,0:T(8,128)}, u32[]{:S(2)}) copy-start(f32[24,2304]{1,0:T(8,128)} %param.26) | copy-start | bytes 663556
  464.9 17.2 %copy-start.38 = (f32[24,2304]{1,0:T(8,128)S(1)}, f32[24,2304]{1,0:T(8,128)}, u32[]{:S(2)}) copy-start(f32[24,2304]{1,0:T(8,128)} %param.27) | copy-start | bytes 663556
  464.9 17.2 %copy-start.39 = (f32[24,2304]{1,0:T(8,128)S(1)}, f32[24,2304]{1,0:T(8,128)}, u32[]{:S(2)}) copy-start(f32[24,2304]{1,0:T(8,128)} %param.28) | copy-start | bytes 663556
  464.9 7.3 %collective-permute-start.24 = (bf16[24,3200]{1,0:T(8,128)(2,1)S(1)}, bf16[24,3200]{1,0:T(8,128)(2,1)S(1)}, u32[]{:S(2)}, u32[]{:S(2)}) collective-permute-start(bf16[24,3200]{1,0:T(8,128)(2,1)S(1)} %slice.263), channel_id=1, source_target_pairs={{0,3},{1,0},{2,1},{3,2},{4,7},{5,4},{6,5},{7,6},{8,11},{9,8},{10,9... | collective-permute-start | bytes 460808 | tf_op jit(solution)/shard_map/ppermute | solution.py:461
  467.9 12.6 %collective-permute-start.28 = (bf16[24,3200]{1,0:T(8,128)(2,1)S(1)}, bf16[24,3200]{1,0:T(8,128)(2,1)S(1)}, u32[]{:S(2)}, u32[]{:S(2)}) collective-permute-start(bf16[24,3200]{1,0:T(8,128)(2,1)S(1)} %get-tuple-element.350), channel_id=1, source_target_pairs={{0,2},{1,3},{2,0},{3,1},{4,6},{5,7},{6,4},{7,5},{8,10},{9,11},{10,... | collective-permute-start | bytes 460808 | tf_op jit(solution)/shard_map/ppermute | solution.py:461
  468.6 11.9 %collective-permute-start.29 = (bf16[24,3200]{1,0:T(8,128)(2,1)S(1)}, bf16[24,3200]{1,0:T(8,128)(2,1)S(1)}, u32[]{:S(2)}, u32[]{:S(2)}) collective-permute-start(bf16[24,3200]{1,0:T(8,128)(2,1)S(1)} %get-tuple-element.351), channel_id=1, source_target_pairs={{0,1},{1,2},{2,3},{3,0},{4,5},{5,6},{6,7},{7,4},{8,9},{9,10},{10,1... | collective-permute-start | bytes 460808 | tf_op jit(solution)/shard_map/ppermute | solution.py:461
  470.9 12.2 %copy-start.37 = (f32[24,768]{1,0:T(8,128)S(1)}, f32[24,768]{1,0:T(8,128)}, u32[]{:S(2)}) copy-start(f32[24,768]{1,0:T(8,128)} %param.29) | copy-start | bytes 221188
  470.9 12.2 %copy-start.42 = (f32[24,768]{1,0:T(8,128)S(1)}, f32[24,768]{1,0:T(8,128)}, u32[]{:S(2)}) copy-start(f32[24,768]{1,0:T(8,128)} %param.30) | copy-start | bytes 221188
  470.9 12.2 %copy-start.43 = (f32[24,768]{1,0:T(8,128)S(1)}, f32[24,768]{1,0:T(8,128)}, u32[]{:S(2)}) copy-start(f32[24,768]{1,0:T(8,128)} %param.31) | copy-start | bytes 221188
  470.9 12.9 %copy-start.49 = (f32[1536]{0:T(1024)S(1)}, f32[1536]{0:T(1024)}, u32[]{:S(2)}) copy-start(f32[1536]{0:T(1024)} %copy-done.48) | copy-start | bytes 18436
  (59 other events, 222.1 us)
